TPU v7x, 32 devices: a whole 2x2x4 slice. The times are simulated.
32 devices in a mesh: seq: 16 (over z, y, core), head: 2 (over x).
Axes of the slice: x: 2, y: 2, z: 4, core: 2. Of those that a mesh axis runs over, the one named last changes fastest.
Arguments:
- query_rows: bfloat16 [4096, 3072], P(('seq', 'head')), may hold values from -16 to 16
- key_rows: bfloat16 [4096, 1024], P(('seq', 'head')), may hold values from -16 to 16
- value_rows: bfloat16 [4096, 1024], P(('seq', 'head')), may hold values from -6 to 6
- residual: bfloat16 [4096, 3072], P(('seq', 'head')), may hold values from -6 to 6
- out_weight: bfloat16 [3072, 3072], P('head'), may hold values from -0.109375 to 0.109375
- gate_table: float32 [64, 3072], replicated, may hold values from -4 to 4
- noise_steps: int32 [8], replicated, may hold values from 0 to 63
- segment_mask: int32 [8, 8], replicated, may hold values from 0 to 1, as said below
- segment_map: int32 [16], replicated, may hold values from 0 to 7, as said below
Outputs:
- layer_output: bfloat16 [4096, 3072], P(('seq', 'head'))
Inputs may be any that keep to these rules, and one draw needn't show every extreme that they name: `segment_mask`: ones on the diagonal, zeros above it. `segment_map`: each segment number stands in exactly 2 entries.
All inputs are finite; a program needn't handle non-finite values.
Results may differ from a plain program's by a relative error of at most 0.0095.
Values may be sent and summed in bfloat16 or wider, within the bound.
No kernel may reach another device: no remote copies, remote signals or barrier semaphores. Data moves between devices by JAX's collectives and lax.ppermute only.
A program may use at most 64 MiB of HBM per device.

v0:
```python
import functools
import math

import jax
import jax.numpy as jnp
from jax import lax
from jax.experimental import pallas as pl
from jax.experimental.pallas import tpu as pltpu
from jax.sharding import PartitionSpec as P

Q_HEADS = 24
KV_HEADS = 8
HEAD_DIM = 128
GROUP = Q_HEADS // KV_HEADS
CORES = 2
UNITS = 2
NEG = -1e30
SCALE = 1.4426950408889634 * HEAD_DIM ** -0.5
STAT = 8
ONES = 16
LARGE = 1e27
VMEM_LIMIT = 24 * 1024 * 1024
LITTLE = pl.CostEstimate(flops=1, bytes_accessed=1, transcendentals=0)


def grid_of(n_seq):
    chips = n_seq // CORES
    inner = 2 ** (int(math.log2(chips)) // 2)
    return chips // inner, inner


def attend_kernel(place, n_items, parts, half, rows, tok, first, last, refs):
    own_ref, map_ref, mask_ref, q_ref = refs[:4]
    mixed = half is not None
    tiles = 1 if mixed else parts
    state_in = None if first else refs[4]
    st_s, qt_s, kv_s, vt_s, list_s, land_s, seen_s, full_s, count_s, top_s, sems = refs[-11:]
    outs = 2 if mixed else 1
    items, outs = refs[4 if first else 5 : -11 - outs], refs[-11 - outs : -11]
    st, qt = st_s if last else outs[0], qt_s if mixed else q_ref
    heads = qt.shape[1]
    kv_heads = heads // GROUP
    kvw = kv_heads * HEAD_DIM
    own = own_ref[0]
    sums = slice(0, HEAD_DIM + STAT)
    weights = slice(HEAD_DIM, HEAD_DIM + STAT)
    point = slice(HEAD_DIM + STAT, HEAD_DIM + 2 * STAT)

    def copies(i, kp, ik):
        pieces = place.refs(items, i, kp)
        size = tok // len(pieces)
        return [
            pltpu.make_async_copy(piece, kv_s.at[ik, pl.ds(j * size, size)], sems.at[ik, j])
            for j, piece in enumerate(pieces)
        ]

    seg_q = [map_ref[place.query(own, j)] for j in range(parts)]
    counts = [jnp.int32(0)] * tiles
    landed = jnp.int32(0)
    for i in range(n_items):
        for kp in range(parts):
            ik = i * parts + kp
            seg_k = [map_ref[src] for src in place.sources(own, i, kp)]
            any_seen = jnp.int32(0)
            for qp in range(parts):
                seen = jnp.int32(0)
                for n in range(2):
                    seen_half = (mask_ref[seg_q[qp], seg_k[n]] > 0).astype(jnp.int32)
                    seen_s[qp, 2 * ik + n] = seen_half
                    seen = jnp.maximum(seen, seen_half)
                any_seen = jnp.maximum(any_seen, seen)
                if not mixed:
                    list_s[qp, counts[qp]] = ik
                    counts[qp] = counts[qp] + seen
            if mixed:
                list_s[0, counts[0]] = ik
                counts[0] = counts[0] + any_seen
            land_s[landed] = ik
            landed = landed + any_seen

            @pl.when(any_seen > 0)
            def _():
                if place.near:
                    pieces = place.refs(items, i, kp)
                    size = tok // len(pieces)
                    for j, piece in enumerate(pieces):
                        kv_s[ik, j * size : (j + 1) * size] = piece[...]
                else:
                    for one in copies(i, kp, ik):
                        one.start()

    ones = jnp.ones((ONES, tok), jnp.bfloat16)

    def land(t, carry):
        ik = land_s[t]
        if not place.near:
            for one in copies(0, 0, ik):
                one.wait()
        for kh in range(kv_heads):
            v = kv_s[ik, :, kvw + kh * HEAD_DIM : kvw + (kh + 1) * HEAD_DIM]
            vt_s[ik, kh, :HEAD_DIM] = v.T
            vt_s[ik, kh, HEAD_DIM:] = ones
        return carry

    lax.fori_loop(0, landed, land, 0)

    def blocks(qp, t):
        single = 2 * t + 1 >= full_s[qp]
        i0 = list_s[qp, 2 * t]
        i1 = list_s[qp, jnp.where(single, 2 * t, 2 * t + 1)]
        if mixed:
            left = lax.broadcasted_iota(jnp.int32, (STAT, rows), 1) < rows // 2
        bias = []
        for i in (i0, i1):
            for n in range(2):
                hidden = [
                    jnp.where(seen_s[part, 2 * i + n] > 0, jnp.float32(0.0), jnp.float32(NEG))
                    for part in ((0, 1) if mixed else (qp,))
                ]
                bias.append(jnp.where(left, hidden[0], hidden[1]) if mixed else hidden[0])
        again = jnp.where(single, jnp.float32(NEG), jnp.float32(0.0))
        bias[2:] = [one + again for one in bias[2:]]
        return i0, i1, bias

    def operands(kh, i0, i1):
        lanes = slice(kh * HEAD_DIM, (kh + 1) * HEAD_DIM)
        return (
            [jnp.concatenate([kv_s[i, :, lanes]] * 2, axis=1) for i in (i0, i1)],
            [vt_s[i, kh] for i in (i0, i1)],
        )

    def slow(units, qp, t):
        i0, i1, bias = blocks(qp, t)
        for h in range(heads):
            kh = h // GROUP
            unit = kh % UNITS
            s0_acc, s1_acc, pv_acc = units[unit]
            keys, values = operands(kh, i0, i1)
            pltpu.matmul_push_rhs(qt[qp, h], 0, unit)
            pltpu.matmul_acc_lhs(s0_acc, keys[0], 0)
            pltpu.matmul_acc_lhs(s1_acc, keys[1])
            s = [pltpu.matmul_pop(acc).reshape(-1, STAT, rows) for acc in (s0_acc, s1_acc)]
            before = st[qp, h, point]
            quarters = [x[n * (tok // 16) : (n + 1) * (tok // 16)] for x in s for n in range(2)]
            top = functools.reduce(jnp.maximum, [jnp.max(x, axis=0) + one for x, one in zip(quarters, bias)])
            now = jnp.maximum(before, jnp.max(top, axis=0, keepdims=True))
            for j, value in enumerate(values):
                p = [jnp.exp2(quarters[2 * j + n] - (now - bias[2 * j + n])[None]) for n in range(2)]
                p = jnp.concatenate(p, axis=0).reshape(tok, rows).astype(jnp.bfloat16)
                pltpu.matmul_push_rhs(p, 1, unit)
                pltpu.matmul_acc_lhs(pv_acc, value, 1)
            kept = st[qp, h, sums].reshape(-1, STAT, rows) * jnp.exp2(before - now)[None]
            st[qp, h, sums] = kept.reshape(-1, rows) + pltpu.matmul_pop(pv_acc)[sums]
            st[qp, h, point] = now

    def fast(units, qp, t):
        i0, i1, bias = blocks(qp, t)
        keys, values = zip(*[operands(kh, i0, i1) for kh in range(kv_heads)])

        def begin(kh, g):
            unit = units[kh % len(units)]
            pltpu.matmul_push_rhs(qt[qp, kh * GROUP + g], 0, kh % len(units))
            pltpu.matmul_acc_lhs(unit[0], keys[kh][0], 0)
            pltpu.matmul_acc_lhs(unit[1], keys[kh][1])

        def weights_of(kh, g, j):
            s = pltpu.matmul_pop(units[kh % len(units)][j]).reshape(-1, STAT, rows)
            ref = st[qp, kh * GROUP + g, point]
            p = [
                jnp.exp2(s[n * (tok // 16) : (n + 1) * (tok // 16)] - (ref - bias[2 * j + n])[None])
                for n in range(2)
            ]
            return jnp.concatenate(p, axis=0).reshape(tok, rows).astype(jnp.bfloat16)

        for first_kh in range(0, kv_heads, len(units)):
            together = range(first_kh, min(first_kh + len(units), kv_heads))
            for kh in together:
                begin(kh, 0)
            for g in range(GROUP):
                p = {(kh, j): weights_of(kh, g, j) for j in range(2) for kh in together}
                if g + 1 < GROUP:
                    for kh in together:
                        begin(kh, g + 1)
                for j in range(2):
                    for kh in together:
                        pltpu.matmul_push_rhs(p[kh, j], 1, kh % len(units))
                        pltpu.matmul_acc_lhs(units[kh % len(units)][2], values[kh][j], 1)
                for kh in together:
                    h = kh * GROUP + g
                    st[qp, h, sums] = st[qp, h, sums] + pltpu.matmul_pop(units[kh % len(units)][2])[sums]

    columns_of = slice(half * rows // 2, (half + 1) * rows // 2) if mixed else slice(0, rows)
    if mixed:
        for h in range(heads):
            qt_s[0, h] = jnp.concatenate([q_ref[part, h, :, columns_of] for part in range(2)], axis=1)
    for qp in range(tiles):
        full_s[qp] = counts[qp]
        count_s[qp] = (counts[qp] + 1) // 2

    def attempt(again, carry):
        @pl.when(jnp.logical_or(again == 0, top_s[0] > 0))
        def _():
            for qp in range(tiles):
                for h in range(heads):
                    if mixed:
                        st[0, h] = jnp.concatenate([state_in[part, h, :, columns_of] for part in range(2)], axis=1)
                    elif first:
                        st[qp, h, sums] = jnp.zeros((HEAD_DIM + STAT, rows), jnp.float32)
                        st[qp, h, point] = jnp.full((STAT, rows), NEG, jnp.float32)
                    else:
                        st[qp, h] = state_in[qp, h]

            def one_part(qp, carry):
                pairs = count_s[qp]
                switch = jnp.where(again > 0, pairs, 1 if first else 0)

                def both(*accs):
                    units = [accs[3 * unit : 3 * unit + 3] for unit in range(UNITS)]

                    def one_slow(t, carry):
                        slow(units, qp, t)
                        return carry

                    def one_fast(t, carry):
                        fast(units, qp, t)
                        return carry

                    lax.fori_loop(0, switch, one_slow, 0)
                    lax.fori_loop(switch, pairs, one_fast, 0)

                accumulators = []
                for unit in range(UNITS):
                    accumulators += [pltpu.ACC(unit)((tok, rows), jnp.float32)] * 2
                    accumulators.append(pltpu.ACC(unit)((HEAD_DIM + ONES, rows), jnp.float32))
                pl.run_scoped(both, *accumulators)
                return carry

            lax.fori_loop(0, tiles, one_part, 0)
            top = jnp.zeros((STAT, rows), jnp.float32)
            for qp in range(tiles):
                for h in range(heads):
                    top = jnp.maximum(top, jnp.where(st[qp, h, weights] < LARGE, 0.0, 1.0))
            top_s[0] = (jnp.max(top) > 0.0).astype(jnp.int32)

        return carry

    top_s[0] = 0
    lax.fori_loop(0, 2, attempt, 0)
    if last:
        for qp in range(tiles):
            for h in range(heads):
                lanes = slice(h * HEAD_DIM, (h + 1) * HEAD_DIM)
                inv = 1.0 / st[qp, h, weights]
                att = st[qp, h, :HEAD_DIM].reshape(-1, STAT, rows) * inv[None]
                att = att.reshape(HEAD_DIM, rows).T.astype(jnp.bfloat16)
                if mixed:
                    outs[0][:, lanes] = att[: rows // 2]
                    outs[1][:, lanes] = att[rows // 2 :]
                else:
                    outs[0][qp * rows : (qp + 1) * rows, lanes] = att


class GridPlace:
    near = True

    def __init__(self, metas, n_a, n_b, tok):
        self.metas, self.n_a, self.n_b, self.tok = metas, n_a, n_b, tok

    def query(self, own, part):
        return (own // CORES) * CORES + (own % CORES + part) % CORES

    def sources(self, own, i, part):
        a, b, c = own // (CORES * self.n_b), (own // CORES) % self.n_b, own % CORES
        return [
            ((a ^ flip) * self.n_b + (b + db) % self.n_b) * CORES + (c + part) % CORES
            for _, _, flip, db in self.metas[i]
        ]

    def refs(self, items, i, part):
        rows = self.tok // 2
        return [items[n].at[pl.ds(base + part * rows, rows)] for n, base, _, _ in self.metas[i]]


class FlatPlace:
    near = False

    def __init__(self, tok):
        self.tok = tok

    def query(self, own, part):
        return own

    def sources(self, own, i, part):
        return [i, i]

    def refs(self, items, i, part):
        return [items[0].at[pl.ds(i * self.tok, self.tok)]]


def other_columns(own, pieces):
    rows, width = pieces[0].shape
    half = width // CORES
    vmem = pl.BlockSpec(memory_space=pltpu.VMEM)

    def kernel(own_ref, *refs):
        lanes = pl.ds(pl.multiple_of((own_ref[0] + 1) % CORES * half, half), half)
        for i, ref in enumerate(refs[:-1]):
            refs[-1][i * rows : (i + 1) * rows] = ref[:, lanes]

    return pl.pallas_call(
        kernel,
        out_shape=jax.ShapeDtypeStruct((len(pieces) * rows, half), pieces[0].dtype),
        in_specs=[pl.BlockSpec(memory_space=pltpu.SMEM)] + [vmem] * len(pieces),
        out_specs=vmem,
        compiler_params=pltpu.CompilerParams(vmem_limit_bytes=VMEM_LIMIT),
        cost_estimate=LITTLE,
        name="other_columns",
    )(own, *pieces)


def moved(kernel, args, shapes, name):
    vmem = pl.BlockSpec(memory_space=pltpu.VMEM)
    return pl.pallas_call(
        kernel,
        out_shape=[jax.ShapeDtypeStruct(shape, jnp.bfloat16) for shape in shapes],
        in_specs=[pl.BlockSpec(memory_space=pltpu.SMEM)] + [vmem] * (len(args) - 1),
        out_specs=[vmem] * len(shapes),
        compiler_params=pltpu.CompilerParams(vmem_limit_bytes=VMEM_LIMIT),
        cost_estimate=LITTLE,
        name=name,
    )(*args)


def joined(own, above, below):
    rows, width = above.shape

    def kernel(own_ref, above_ref, below_ref, out_ref):
        out_ref[:rows] = above_ref[...]
        out_ref[rows:] = below_ref[...]

    return moved(kernel, (own, above, below), [(2 * rows, width)], "joined")[0]


def lower_half(own, x):
    rows, width = x.shape

    def kernel(own_ref, x_ref, out_ref):
        out_ref[...] = x_ref[rows // 2 :]

    return moved(kernel, (own, x), [(rows // 2, width)], "lower_half")[0]


def picked(own, at_ends, at_middle, n_a, n_b):
    rows, width = at_ends.shape

    def kernel(own_ref, ends_ref, middle_ref, whole_ref, half_ref):
        a = own_ref[0] // (CORES * n_b)
        at_end = jnp.logical_or(a == 0, a == n_a - 1)

        def take(ref):
            whole_ref[...] = ref[...]
            half_ref[...] = ref[: rows // 2]

        pl.when(at_end)(lambda: take(ends_ref))
        pl.when(jnp.logical_not(at_end))(lambda: take(middle_ref))

    return moved(kernel, (own, at_ends, at_middle), [(rows, width), (rows // 2, width)], "picked")


def turn(own, parts):
    pieces = [x for part in parts for x in part]
    heads = min(x.shape[1] for x in pieces) // HEAD_DIM
    rows = sum(x.shape[0] for x in parts[0])
    vmem = pl.BlockSpec(memory_space=pltpu.VMEM)

    def kernel(own_ref, *refs):
        begin = own_ref[0] % CORES * heads * HEAD_DIM
        at = 0
        for qp, part in enumerate(parts):
            some = refs[at : at + len(part)]
            at += len(part)
            for h in range(heads):
                turned = []
                for ref in some:
                    first = h * HEAD_DIM
                    if ref.shape[1] > heads * HEAD_DIM:
                        first = pl.multiple_of(begin + first, HEAD_DIM)
                    turned.append(ref[:, pl.ds(first, HEAD_DIM)].astype(jnp.float32).T)
                scaled = jnp.concatenate(turned, axis=1) * SCALE
                high = scaled.astype(jnp.bfloat16)
                refs[-1][qp, h, :HEAD_DIM] = high
                refs[-1][qp, h, HEAD_DIM:] = (scaled - high.astype(jnp.float32)).astype(jnp.bfloat16)

    return pl.pallas_call(
        kernel,
        out_shape=pltpu.VMEM((len(parts), heads, 2 * HEAD_DIM, rows), jnp.bfloat16),
        in_specs=[pl.BlockSpec(memory_space=pltpu.SMEM)] + [vmem] * len(pieces),
        out_specs=vmem,
        compiler_params=pltpu.CompilerParams(vmem_limit_bytes=VMEM_LIMIT),
        cost_estimate=LITTLE,
        name="turn",
    )(own, *pieces)


def attend(scalars, q, state, arrays, place, n_items, parts, tok, last, half=None):
    first = state is None
    heads, rows = q.shape[1], q.shape[3]
    width = arrays[0].shape[1]
    smem = pl.BlockSpec(memory_space=pltpu.SMEM)
    vmem = pl.BlockSpec(memory_space=pltpu.VMEM)
    args = list(scalars) + [pinned(q)] + ([] if first else [pinned(state)])
    args += [pinned(x) if place.near else x for x in arrays]
    specs = [smem] * 3 + [vmem] + ([] if first else [vmem])
    specs += [vmem if place.near else pl.BlockSpec(memory_space=pl.ANY)] * len(arrays)
    shape = (parts, heads, HEAD_DIM + 2 * STAT, rows)
    tile_shape = shape if half is None else (1,) + shape[1:]
    blocks = n_items * parts
    scratch = [
        pltpu.VMEM(tile_shape if last else (STAT, HEAD_DIM), jnp.float32),
        pltpu.VMEM((1,) + q.shape[1:] if half is not None else (ONES, HEAD_DIM), jnp.bfloat16),
        pltpu.VMEM((blocks, tok, width), jnp.bfloat16),
        pltpu.VMEM((blocks, heads // GROUP, HEAD_DIM + ONES, tok), jnp.bfloat16),
        pltpu.SMEM((parts, blocks + 1), jnp.int32),
        pltpu.SMEM((blocks + 1,), jnp.int32),
        pltpu.SMEM((parts, 2 * blocks), jnp.int32),
        pltpu.SMEM((parts,), jnp.int32),
        pltpu.SMEM((parts,), jnp.int32),
        pltpu.SMEM((1,), jnp.int32),
        pltpu.SemaphoreType.DMA((blocks, 2)),
    ]
    if last:
        out_shape = [jax.ShapeDtypeStruct((parts * rows, heads * HEAD_DIM), jnp.bfloat16)]
        if half is not None:
            out_shape = [jax.ShapeDtypeStruct((rows // 2, heads * HEAD_DIM), jnp.bfloat16)] * 2
    else:
        out_shape = [pltpu.VMEM(shape, jnp.float32)]

    def kernel(*refs):
        attend_kernel(place, n_items, parts, half, rows, tok, first, last, refs)

    return pl.pallas_call(
        kernel,
        out_shape=out_shape,
        in_specs=specs,
        out_specs=[vmem] * len(out_shape),
        scratch_shapes=scratch,
        compiler_params=pltpu.CompilerParams(vmem_limit_bytes=VMEM_LIMIT),
        cost_estimate=LITTLE,
        name="attend",
    )(*args)


def pinned(x):
    return pltpu.with_memory_space_constraint(x, pltpu.VMEM)


def fetch(weight):
    chunks = 12
    rows = weight.shape[0] // chunks

    def kernel(weight_ref, out_ref, sems):
        copies = [
            pltpu.make_async_copy(
                weight_ref.at[pl.ds(i * rows, rows)], out_ref.at[pl.ds(i * rows, rows)], sems.at[i]
            )
            for i in range(chunks)
        ]
        for one in copies:
            one.start()
        for one in copies:
            one.wait()

    return pl.pallas_call(
        kernel,
        out_shape=pltpu.VMEM(weight.shape, weight.dtype),
        in_specs=[pl.BlockSpec(memory_space=pltpu.HBM)],
        out_specs=pl.BlockSpec(memory_space=pltpu.VMEM),
        scratch_shapes=[pltpu.SemaphoreType.DMA((chunks,))],
        compiler_params=pltpu.CompilerParams(vmem_limit_bytes=VMEM_LIMIT),
        cost_estimate=LITTLE,
        name="fetch",
    )(pltpu.with_memory_space_constraint(weight, pltpu.HBM))


def project(own, parts, weight, rows, partial=None, ending=None):
    width = weight.shape[1]
    depth = parts[0][0].shape[1]
    tile = math.gcd(width, 512)
    smem = pl.BlockSpec(memory_space=pltpu.SMEM)
    vmem = pl.BlockSpec(memory_space=pltpu.VMEM)
    n = len(parts)
    args = [own] + [x for x, _, _ in parts] + [pinned(weight)]
    specs = [smem] + [vmem] * (n + 1)
    scratch = []
    out_shape = [jax.ShapeDtypeStruct((rows, width), jnp.bfloat16)]
    if partial is not None:
        args.append(pinned(partial))
        specs.append(vmem)
    elif ending is not None:
        args += list(ending)
        args[-2] = pltpu.with_memory_space_constraint(args[-2], pltpu.HBM)
        specs += [smem] * 2 + [pl.BlockSpec(memory_space=pltpu.HBM), vmem]
        out_shape = [pltpu.VMEM((rows, width), jnp.float32), pltpu.VMEM((STAT, width), jnp.float32)]
        scratch = [pltpu.VMEM((STAT, width), jnp.float32), pltpu.SemaphoreType.DMA]
    else:
        out_shape = [pltpu.VMEM((rows, width), jnp.float32)]

    def kernel(*refs):
        own_ref, part_refs, weight_ref, refs = refs[0], refs[1 : n + 1], refs[n + 1], refs[n + 2 :]
        if ending is not None:
            steps_ref, map_ref, gate_ref, residual_ref, out_ref, row_ref, near, sem = refs
            step = steps_ref[map_ref[own_ref[0]]]
            copy = pltpu.make_async_copy(
                gate_ref.at[pl.ds(pl.multiple_of((step // STAT) * STAT, STAT), STAT)], near, sem
            )
            copy.start()
            copy.wait()
            chosen = lax.broadcasted_iota(jnp.int32, (STAT, width), 0) == step % STAT
            row = jnp.sum(jnp.where(chosen, near[...], 0.0), axis=0, keepdims=True)
            row_ref[...] = jnp.broadcast_to(row, (STAT, width))
        else:
            out_ref = refs[-1]

        def one(t, carry):
            lanes = pl.ds(pl.multiple_of(t * tile, tile), tile)
            total = None
            for j in range(n):
                first_row = parts[j][2]
                group = (own_ref[0] + parts[j][1]) % CORES
                weight_rows = pl.ds(pl.multiple_of(group * depth, depth), depth)
                term = jnp.dot(
                    part_refs[j][first_row : first_row + rows],
                    weight_ref[weight_rows, lanes],
                    preferred_element_type=jnp.float32,
                )
                total = term if total is None else total + term
            if partial is not None:
                total = total + refs[0][:, lanes]
            if ending is not None:
                gate = jnp.concatenate([row_ref[:, lanes]] * (rows // STAT), axis=0)
                total = residual_ref[:, lanes].astype(jnp.float32) + gate * total
            out_ref[:, lanes] = total.astype(out_ref.dtype)
            return carry

        lax.fori_loop(0, width // tile, one, 0)

    return pl.pallas_call(
        kernel,
        out_shape=out_shape,
        in_specs=specs,
        out_specs=[vmem] * len(out_shape),
        scratch_shapes=scratch,
        compiler_params=pltpu.CompilerParams(vmem_limit_bytes=VMEM_LIMIT),
        cost_estimate=pl.CostEstimate(
            flops=2 * rows * depth * n * width, bytes_accessed=2 * depth * n * width, transcendentals=0
        ),
        name="project",
    )(*args)


def columns(x, part, width):
    return lax.dynamic_slice_in_dim(x, part * width, width, 1)


def paired(query_rows, key_rows, value_rows, out_weight, scalars, ending, n_a, n_b):
    n_seq = n_a * n_b * CORES
    groups = 2 * CORES
    own = scalars[0]
    kvw = key_rows.shape[1] // groups
    rows = query_rows.shape[0]
    tok = 2 * rows
    x = lax.axis_index("head")
    c = lax.axis_index("seq") % CORES

    def index(a, b, k):
        return (a * n_b + b) * CORES + k

    def swapped(piece, dx, dc):
        pairs = [
            ((s ^ dc) * 2 + (h ^ dx), s * 2 + h) for s in range(n_seq) for h in range(2)
        ]
        return lax.ppermute(piece, ("seq", "head"), pairs)

    def along_a(piece, moves):
        pairs = [
            (index(a, b, k), index(to, b, k)) for a, to in moves for b in range(n_b) for k in range(CORES)
        ]
        return lax.ppermute(piece, "seq", pairs)

    def beside_of(piece, only):
        pairs = [
            (index(a, 1 - b, k), index(a, b, k)) for a in only for b in range(n_b) for k in range(CORES)
        ]
        return lax.ppermute(piece, "seq", pairs)

    def stage(state, q, arrays, metas, last=False, half=None):
        return attend(
            scalars, q, state, arrays, GridPlace(metas, n_a, n_b, tok), len(metas), CORES, tok, last, half
        )

    def halves_of(first, base, flip, db):
        if isinstance(first, int):
            return [(first, base, flip, db), (first, base + tok, flip, db)]
        return [(n, base, flip, db) for n in first]

    def kv_for(dx, dc):
        j = (x ^ dx) * CORES + (c ^ dc)
        return jnp.concatenate([columns(key_rows, j, kvw), columns(value_rows, j, kvw)], axis=1)

    chips = list(range(n_a))
    order = [(0, 0), (1, 0), (0, 1), (1, 1)]
    pieces = {d: kv_for(*d) if sum(d) == 0 else swapped(kv_for(*d), *d) for d in order}
    early = jnp.concatenate([pieces[0, 0], pieces[0, 1]], axis=0)
    later = jnp.concatenate([pieces[1, 0], pieces[1, 1]], axis=0)
    block = jnp.concatenate([early, later], axis=0)
    qw = query_rows.shape[1] // 2
    q_own, q_other = columns(query_rows, x, qw), columns(query_rows, 1 - x, qw)
    block, early, later, out_weight, q_own, q_other = lax.optimization_barrier(
        (block, early, later, out_weight, q_own, q_other)
    )
    by_one, by_two = [(a, a ^ 1) for a in chips], [(a, a ^ 2) for a in chips]
    beside = beside_of(block, chips)
    next_early, far_early = along_a(early, by_one), along_a(early, by_two)
    q_came = swapped(q_other, 1, 0)
    weight = fetch(out_weight)
    beside, next_early, far_early, q_came, weight = lax.optimization_barrier(
        (beside, next_early, far_early, q_came, weight)
    )
    beside_early = beside_of(joined(own, next_early, far_early), chips)
    next_later, far_later = along_a(later, by_one), along_a(later, by_two)
    q_core = swapped(other_columns(own, [q_own, q_came]), 0, 1)
    q = turn(own, [[q_own, q_came], [q_core]])
    (state,) = stage(None, q, [block, beside], [halves_of(0, 0, 0, 0), halves_of(1, 0, 0, 1)])
    again, state = lax.optimization_barrier((block, state))
    to_middle = along_a(again, [(1, 2), (2, 1)])
    next_later, far_later, beside_early, state = lax.optimization_barrier(
        (next_later, far_later, beside_early, state)
    )
    beside_later = beside_of(joined(own, next_later, far_later), chips)
    to_ends = along_a(joined(own, far_early, far_later), [(1, 0), (2, 3)])
    (state,) = stage(
        state, q, [next_early, next_later, far_early, far_later],
        [halves_of((0, 1), 0, 1, 0), halves_of((2, 3), 0, 2, 0)],
    )
    to_middle, state = lax.optimization_barrier((to_middle, state))
    (state,) = stage(state, q, [beside_early], [[(0, 0, 1, 1), (0, tok, 2, 1)]])
    to_ends, to_middle, beside_later, state = lax.optimization_barrier((to_ends, to_middle, beside_later, state))
    last, last_upper = picked(own, to_ends, to_middle, n_a, n_b)
    beside_last = [beside_of(last_upper, chips), along_a(lower_half(own, beside_later), by_one)]
    (state,) = stage(
        state, q, [beside_later, last], [[(0, 0, 1, 1), (0, tok, 2, 1)], halves_of(1, 0, 3, 0)]
    )
    last_block = [halves_of((0, 1), 0, 3, 1)]
    kept, sent = stage(state, q, beside_last, last_block, True, 1)
    came = swapped(sent, 0, 1)
    (begun,) = project(own, [(kept, 0, 0)], weight, rows)
    (theirs,) = project(own, [(came, 1, 0)], weight, rows, partial=begun)
    came_back = lax.ppermute(theirs, "head", [(0, 1), (1, 0)])
    state, theirs = lax.optimization_barrier((state, theirs))
    kept, sent = stage(state, q, beside_last, last_block, True, 0)
    came = swapped(sent, 0, 1)
    base, gate = project(own, [(kept, 0, 0), (came, 1, 0)], weight, rows, ending=ending)
    return (base + gate[:1] * came_back.astype(jnp.float32)).astype(jnp.bfloat16)


def gathered_attention(query_rows, key_rows, value_rows, scalars):
    spread = functools.partial(lax.all_to_all, axis_name="head", split_axis=1, concat_axis=0, tiled=True)
    local = jnp.concatenate([spread(key_rows), spread(value_rows)], axis=1)
    every = lax.all_gather(local, "seq", axis=0, tiled=True)
    tok = local.shape[0]
    return attend(
        scalars, turn(scalars[0], [[spread(query_rows)]]), None, [every], FlatPlace(tok), every.shape[0] // tok, 1, tok, True
    )[0]


def per_device(
    query_rows,
    key_rows,
    value_rows,
    residual,
    out_weight,
    gate_table,
    noise_steps,
    segment_mask,
    segment_map,
):
    n_seq = lax.axis_size("seq")
    n_head = lax.axis_size("head")
    own_seq = lax.axis_index("seq").astype(jnp.int32)
    own = own_seq.reshape(1)
    scalars = (own, segment_map, segment_mask)
    n_a, n_b = grid_of(n_seq)
    if n_head == 2 and n_a == 4 and n_b == 2:
        ending = (noise_steps, segment_map, gate_table, residual)
        return paired(query_rows, key_rows, value_rows, out_weight, scalars, ending, n_a, n_b)
    attended = gathered_attention(query_rows, key_rows, value_rows, scalars)
    projected = lax.psum_scatter(
        jnp.dot(attended, out_weight, preferred_element_type=jnp.float32).astype(jnp.bfloat16),
        "head",
        scatter_dimension=0,
        tiled=True,
    ).astype(jnp.float32)
    gate_row = lax.dynamic_slice_in_dim(gate_table, noise_steps[segment_map[own_seq]], 1, 0)
    return (residual.astype(jnp.float32) + gate_row * projected).astype(jnp.bfloat16)


def solution(mesh):
    placed = (
        P(("seq", "head"), None),
        P(("seq", "head"), None),
        P(("seq", "head"), None),
        P(("seq", "head"), None),
        P("head", None),
        P(),
        P(),
        P(),
        P(),
    )
    return jax.shard_map(
        per_device, mesh=mesh, in_specs=placed, out_specs=P(("seq", "head"), None), check_vma=False
    )
```

profile of v0, /device:TPU:0, one launch (start us, length us, event | category | flops | bytes accessed | tf_op | source)
XLA Modules:
  0.0 95.4 jit_solution(7937994571003441550)
XLA Ops:
  0.0 0.0 copy-start.4
  0.0 1.2 %constant_dynamic-slice_fusion.8 = (bf16[128,256]{1,0:T(8,128)(2,1)S(1)}, bf16[128,256]{1,0:T(8,128)(2,1)S(1)}, bf16[128,256]{1,0:T(8,128)(2,1)S(1)}, bf16[128,2...) fusion(bf16[128,1024]{1,0:T(8,128)(2,1)} %param.11, ...), kind=kLoop, calls=%fused_computation.15 | loop fusion | bytes 1048592 | tf_op jit(solution)/shard_map/dynamic_slice | solution.py:562
  1.2 3.0 %collective-permute-start.1 = (bf16[128,512]{1,0:T(8,128)(2,1)S(1)}, bf16[128,512]{1,0:T(8,128)(2,1)S(1)}, u32[]{:S(2)}, u32[]{:S(2)}) collective-permute-start(bf16[128,512]{1,0:T(8,128)(2,1)S(1)} %pad_maximum_fusion.4), channel_id=1, source_target_pairs={{1,0},{0,1},{3,2},{2,3},{5,4},{4,5},{7,6},{6,7},{9,8},{8,9},{11,10... | collective-permute-start | bytes 393224 | tf_op jit(solution)/shard_map/ppermute | solution.py:582
  4.2 0.1 collective-permute-start.2
  4.3 0.2 collective-permute-start
  4.5 0.0 copy-done.4
  4.5 0.1 constant_dynamic-slice_fusion
  4.6 1.2 %collective-permute-done = bf16[128,512]{1,0:T(8,128)(2,1)S(1)} collective-permute-done((bf16[128,512]{1,0:T(8,128)(2,1)S(1)}, bf16[128,512]{1,0:T(8,128)(2,1)S(1)}, u32[]{:S(2)}, u32[]{:S(2)}) %collective-permute-start) | collective-permute-done | bytes 131104 | tf_op jit(solution)/shard_map/ppermute | solution.py:582
  5.8 2.4 %collective-permute-done.1 = bf16[128,512]{1,0:T(8,128)(2,1)S(1)} collective-permute-done((bf16[128,512]{1,0:T(8,128)(2,1)S(1)}, bf16[128,512]{1,0:T(8,128)(2,1)S(1)}, u32[]{:S(2)}, u32[]{:S(2)}) %collective-permute-start.1) | collective-permute-done | bytes 131104 | tf_op jit(solution)/shard_map/ppermute | solution.py:582
  8.1 2.0 %collective-permute-done.2 = bf16[128,512]{1,0:T(8,128)(2,1)S(1)} collective-permute-done((bf16[128,512]{1,0:T(8,128)(2,1)S(1)}, bf16[128,512]{1,0:T(8,128)(2,1)S(1)}, u32[]{:S(2)}, u32[]{:S(2)}) %collective-permute-start.2) | collective-permute-done | bytes 131104 | tf_op jit(solution)/shard_map/ppermute | solution.py:582
  10.2 1.5 %collective-permute-start.3 = (bf16[512,512]{1,0:T(8,128)(2,1)S(1)}, bf16[512,512]{1,0:T(8,128)(2,1)S(1)}, u32[]{:S(2)}, u32[]{:S(2)}) collective-permute-start(bf16[512,512]{1,0:T(8,128)(2,1)S(1)} %pad_maximum_fusion.refs_4_), channel_id=1, source_target_pairs={{4,0},{6,2},{0,4},{2,6},{12,8},{14,10},{8,12},{10,14},{20,16},{22,... | collective-permute-start | bytes 1572872 | tf_op jit(solution)/shard_map/ppermute | solution.py:594
  11.7 1.0 %collective-permute-start.6 = (bf16[128,1536]{1,0:T(8,128)(2,1)S(1)}, bf16[128,1536]{1,0:T(8,128)(2,1)S(1)}, u32[]{:S(2)}, u32[]{:S(2)}) collective-permute-start(bf16[128,1536]{1,0:T(8,128)(2,1)S(1)} %get-tuple-element.40), channel_id=1, source_target_pairs={{1,0},{0,1},{3,2},{2,3},{5,4},{4,5},{7,6},{6,7},{9,8},{8,9},{11,10... | collective-permute-start | bytes 1179656 | tf_op jit(solution)/shard_map/ppermute | solution.py:582
  12.7 2.6 %collective-permute-start.5 = (bf16[256,512]{1,0:T(8,128)(2,1)S(1)}, bf16[256,512]{1,0:T(8,128)(2,1)S(1)}, u32[]{:S(2)}, u32[]{:S(2)}) collective-permute-start(bf16[256,512]{1,0:T(8,128)(2,1)S(1)} %pad_maximum_fusion.1), channel_id=1, source_target_pairs={{0,16},{2,18},{4,20},{6,22},{8,24},{10,26},{12,28},{14,30},{16,0},... | collective-permute-start | bytes 786440 | tf_op jit(solution)/shard_map/ppermute | solution.py:588
  15.3 1.6 %collective-permute-start.4 = (bf16[256,512]{1,0:T(8,128)(2,1)S(1)}, bf16[256,512]{1,0:T(8,128)(2,1)S(1)}, u32[]{:S(2)}, u32[]{:S(2)}) collective-permute-start(bf16[256,512]{1,0:T(8,128)(2,1)S(1)} %pad_maximum_fusion.1), channel_id=1, source_target_pairs={{0,8},{2,10},{4,12},{6,14},{8,0},{10,2},{12,4},{14,6},{16,24},{18,... | collective-permute-start | bytes 786440 | tf_op jit(solution)/shard_map/ppermute | solution.py:588
  16.9 3.8 %fetch.1.refs_2_.refs_3_ = bf16[1536,3072]{1,0:T(8,128)(2,1)S(1)} custom-call(bf16[1536,3072]{1,0:T(8,128)(2,1)} %weight_ref), custom_call_target="tpu_custom_call" | custom-call | flops 1 | bytes 1 | tf_op jit(solution)/shard_map/fetch/pallas_call | solution.py:473
  20.7 7.3 %collective-permute-done.5.below_ref.above_ref.refs_7_ = bf16[256,512]{1,0:T(8,128)(2,1)S(1)} collective-permute-done((bf16[256,512]{1,0:T(8,128)(2,1)S(1)}, bf16[256,512]{1,0:T(8,128)(2,1)S(1)}, u32[]{:S(2)}, u32[]{:S(2)}) %collective-permute-start.5) | collective-permute-done | bytes 262176 | tf_op jit(solution)/shard_map/ppermute | solution.py:588
  28.0 0.2 collective-permute-done.4.above_ref.refs_5_
  28.2 0.0 collective-permute-done.6.refs_1_
  28.2 0.0 collective-permute-done.3.refs_5_
  28.3 0.6 collective-permute-start.10
  28.9 0.0 copy-start.1
  28.9 0.0 copy-start.2
  28.9 0.1 collective-permute-start.7
  29.0 1.4 %collective-permute-start.9 = (bf16[256,512]{1,0:T(8,128)(2,1)S(1)}, bf16[256,512]{1,0:T(8,128)(2,1)S(1)}, u32[]{:S(2)}, u32[]{:S(2)}) collective-permute-start(bf16[256,512]{1,0:T(8,128)(2,1)S(1)} %pad_maximum_fusion.2), channel_id=1, source_target_pairs={{0,16},{2,18},{4,20},{6,22},{8,24},{10,26},{12,28},{14,30},{16,0},... | collective-permute-start | bytes 786440 | tf_op jit(solution)/shard_map/ppermute | solution.py:588
  30.3 2.4 %collective-permute-start.8 = (bf16[256,512]{1,0:T(8,128)(2,1)S(1)}, bf16[256,512]{1,0:T(8,128)(2,1)S(1)}, u32[]{:S(2)}, u32[]{:S(2)}) collective-permute-start(bf16[256,512]{1,0:T(8,128)(2,1)S(1)} %pad_maximum_fusion.2), channel_id=1, source_target_pairs={{0,8},{2,10},{4,12},{6,14},{8,0},{10,2},{12,4},{14,6},{16,24},{18,... | collective-permute-start | bytes 786440 | tf_op jit(solution)/shard_map/ppermute | solution.py:588
  32.8 0.0 collective-permute-done.7.refs_2_
  32.8 0.4 turn.1.refs_3_
  33.2 0.0 copy-done.1
  33.2 0.0 copy-done.2
  33.2 6.0 %attend.6.refs_4_ = f32[2,6,144,256]{3,2,1,0:T(8,128)S(1)} custom-call(s32[1]{0:T(128)} %bitcast.own_ref.refs_0_, s32[16]{0:T(128)S(1)} %copy-done.2, s32[8,8]{1,0:T(8,128)S(1)} %copy-done.1, bf16[2,6,256,256]{3,2,1,0:T(8,128)(2,1)S(1)} %turn.1.refs_3_, bf16[512,512]{1,0:T(8,128)(2,1)S(1)} %pad_maximum_fusion.refs_4_, ...), custom_call_target="tpu_custom_call" | custom-call | flops 1 | bytes 1 | tf_op jit(solution)/shard_map/attend/pallas_call | solution.py:441
  39.3 0.7 collective-permute-start.12
  40.0 4.7 %collective-permute-done.9.below_ref.refs_8_ = bf16[256,512]{1,0:T(8,128)(2,1)S(1)} collective-permute-done((bf16[256,512]{1,0:T(8,128)(2,1)S(1)}, bf16[256,512]{1,0:T(8,128)(2,1)S(1)}, u32[]{:S(2)}, u32[]{:S(2)}) %collective-permute-start.9) | collective-permute-done | bytes 262176 | tf_op jit(solution)/shard_map/ppermute | solution.py:588
  44.6 0.0 collective-permute-done.8.refs_6_.above_ref
  44.6 0.0 collective-permute-done.10.refs_5_
  44.7 1.3 %collective-permute-start.11 = (bf16[512,512]{1,0:T(8,128)(2,1)S(1)}, bf16[512,512]{1,0:T(8,128)(2,1)S(1)}, u32[]{:S(2)}, u32[]{:S(2)}) collective-permute-start(bf16[512,512]{1,0:T(8,128)(2,1)S(1)} %joined.4), channel_id=1, source_target_pairs={{8,0},{10,2},{12,4},{14,6},{16,24},{18,26},{20,28},{22,30},{9,1},{... | collective-permute-start | bytes 1572872 | tf_op jit(solution)/shard_map/ppermute | solution.py:588
  46.0 1.1 %collective-permute-start.13 = (bf16[512,512]{1,0:T(8,128)(2,1)S(1)}, bf16[512,512]{1,0:T(8,128)(2,1)S(1)}, u32[]{:S(2)}, u32[]{:S(2)}) collective-permute-start(bf16[512,512]{1,0:T(8,128)(2,1)S(1)} %joined.5), channel_id=1, source_target_pairs={{4,0},{6,2},{0,4},{2,6},{12,8},{14,10},{8,12},{10,14},{20,16},{22,... | collective-permute-start | bytes 1572872 | tf_op jit(solution)/shard_map/ppermute | solution.py:594
  47.2 5.3 %attend.7.refs_4_ = f32[2,6,144,256]{3,2,1,0:T(8,128)S(1)} custom-call(s32[1]{0:T(128)} %bitcast.own_ref.refs_0_, s32[16]{0:T(128)S(1)} %copy-done.2, s32[8,8]{1,0:T(8,128)S(1)} %copy-done.1, bf16[2,6,256,256]{3,2,1,0:T(8,128)(2,1)S(1)} %turn.1.refs_3_, f32[2,6,144,256]{3,2,1,0:T(8,128)S(1)} %attend.6.refs_4_, ...), custom_call_target="tpu_custom_call" | custom-call | flops 1 | bytes 1 | tf_op jit(solution)/shard_map/attend/pallas_call | solution.py:441
  52.4 0.0 collective-permute-done.12.middle_ref
  52.5 2.5 %attend.8.refs_4_ = f32[2,6,144,256]{3,2,1,0:T(8,128)S(1)} custom-call(s32[1]{0:T(128)} %bitcast.own_ref.refs_0_, s32[16]{0:T(128)S(1)} %copy-done.2, s32[8,8]{1,0:T(8,128)S(1)} %copy-done.1, bf16[2,6,256,256]{3,2,1,0:T(8,128)(2,1)S(1)} %turn.1.refs_3_, f32[2,6,144,256]{3,2,1,0:T(8,128)S(1)} %attend.7.refs_4_, ...), custom_call_target="tpu_custom_call" | custom-call | flops 1 | bytes 1 | tf_op jit(solution)/shard_map/attend/pallas_call | solution.py:441
  55.0 4.7 %collective-permute-done.11.ends_ref = bf16[512,512]{1,0:T(8,128)(2,1)S(1)} collective-permute-done((bf16[512,512]{1,0:T(8,128)(2,1)S(1)}, bf16[512,512]{1,0:T(8,128)(2,1)S(1)}, u32[]{:S(2)}, u32[]{:S(2)}) %collective-permute-start.11) | collective-permute-done | bytes 524320 | tf_op jit(solution)/shard_map/ppermute | solution.py:588
  59.6 0.0 collective-permute-done.13.refs_5_.x_ref
  59.6 0.1 picked.1
  59.7 1.6 %collective-permute-start.14 = (bf16[256,512]{1,0:T(8,128)(2,1)S(1)}, bf16[256,512]{1,0:T(8,128)(2,1)S(1)}, u32[]{:S(2)}, u32[]{:S(2)}) collective-permute-start(bf16[256,512]{1,0:T(8,128)(2,1)S(1)} %get-tuple-element.60), channel_id=1, source_target_pairs={{4,0},{6,2},{0,4},{2,6},{12,8},{14,10},{8,12},{10,14},{20,16},{22,... | collective-permute-start | bytes 786440 | tf_op jit(solution)/shard_map/ppermute | solution.py:594
  61.3 2.0 %collective-permute-start.15 = (bf16[256,512]{1,0:T(8,128)(2,1)S(1)}, bf16[256,512]{1,0:T(8,128)(2,1)S(1)}, u32[]{:S(2)}, u32[]{:S(2)}) collective-permute-start(bf16[256,512]{1,0:T(8,128)(2,1)S(1)} %lower_half.1), channel_id=1, source_target_pairs={{0,8},{2,10},{4,12},{6,14},{8,0},{10,2},{12,4},{14,6},{16,24},{18,... | collective-permute-start | bytes 786440 | tf_op jit(solution)/shard_map/ppermute | solution.py:588
  63.3 2.8 %attend.9.refs_4_ = f32[2,6,144,256]{3,2,1,0:T(8,128)S(1)} custom-call(s32[1]{0:T(128)} %bitcast.own_ref.refs_0_, s32[16]{0:T(128)S(1)} %copy-done.2, s32[8,8]{1,0:T(8,128)S(1)} %copy-done.1, bf16[2,6,256,256]{3,2,1,0:T(8,128)(2,1)S(1)} %turn.1.refs_3_, f32[2,6,144,256]{3,2,1,0:T(8,128)S(1)} %attend.8.refs_4_, ...), custom_call_target="tpu_custom_call" | custom-call | flops 1 | bytes 1 | tf_op jit(solution)/shard_map/attend/pallas_call | solution.py:441
  66.0 0.5 collective-permute-done.14.refs_5_
  66.5 1.5 %collective-permute-done.15.refs_6_ = bf16[256,512]{1,0:T(8,128)(2,1)S(1)} collective-permute-done((bf16[256,512]{1,0:T(8,128)(2,1)S(1)}, bf16[256,512]{1,0:T(8,128)(2,1)S(1)}, u32[]{:S(2)}, u32[]{:S(2)}) %collective-permute-start.15) | collective-permute-done | bytes 262176 | tf_op jit(solution)/shard_map/ppermute | solution.py:588
  68.1 2.7 %attend.10 = (bf16[128,768]{1,0:T(8,128)(2,1)S(1)}, bf16[128,768]{1,0:T(8,128)(2,1)S(1)}) custom-call(s32[1]{0:T(128)} %bitcast.own_ref.refs_0_, s32[16]{0:T(128)S(1)} %copy-done.2, s32[8,8]{1,0:T(8,128)S(1)} %copy-done.1, bf16[2,6,256,256]{3,2,1,0:T(8,128)(2,1)S(1)} %turn.1.refs_3_, f32[2,6,144,256]{3,2,1,0:T(8,128)S(1)} %attend.9.refs_4_, ...), custom_call_target="tpu_custom_call" | custom-call | flops 1 | bytes 1 | tf_op jit(solution)/shard_map/attend/pallas_call | solution.py:441
  70.7 0.1 collective-permute-start.16
  70.8 1.7 %project.3.refs_3_ = f32[128,3072]{1,0:T(8,128)S(1)} custom-call(s32[1]{0:T(128)} %bitcast.own_ref.refs_0_, bf16[128,768]{1,0:T(8,128)(2,1)S(1)} %get-tuple-element.63.refs_1_, bf16[1536,3072]{1,0:T(8,128)(2,1)S(1)} %fetch.1.refs_2_.refs_3_), custom_call_target="tpu_custom_call" | custom-call | flops 603979776 | bytes 4718592 | tf_op jit(solution)/shard_map/project/pallas_call | solution.py:547
  72.5 0.0 collective-permute-done.16.refs_1_
  72.5 1.7 %project.4 = bf16[128,3072]{1,0:T(8,128)(2,1)S(1)} custom-call(s32[1]{0:T(128)} %bitcast.own_ref.refs_0_, bf16[128,768]{1,0:T(8,128)(2,1)S(1)} %collective-permute-done.16.refs_1_, bf16[1536,3072]{1,0:T(8,128)(2,1)S(1)} %fetch.1.refs_2_.refs_3_, f32[128,3072]{1,0:T(8,128)S(1)} %project.3.refs_3_), custom_call_target="tpu_custom_call" | custom-call | flops 603979776 | bytes 4718592 | tf_op jit(solution)/shard_map/project/pallas_call | solution.py:547
  74.3 0.0 copy-start
  74.3 0.0 copy-start.3
  74.3 0.6 collective-permute-start.18
  74.9 2.7 %attend.11 = (bf16[128,768]{1,0:T(8,128)(2,1)S(1)}, bf16[128,768]{1,0:T(8,128)(2,1)S(1)}) custom-call(s32[1]{0:T(128)} %bitcast.own_ref.refs_0_, s32[16]{0:T(128)S(1)} %copy-done.2, s32[8,8]{1,0:T(8,128)S(1)} %copy-done.1, bf16[2,6,256,256]{3,2,1,0:T(8,128)(2,1)S(1)} %turn.1.refs_3_, f32[2,6,144,256]{3,2,1,0:T(8,128)S(1)} %attend.9.refs_4_, ...), custom_call_target="tpu_custom_call" | custom-call | flops 1 | bytes 1 | tf_op jit(solution)/shard_map/attend/pallas_call | solution.py:441
  77.5 0.3 collective-permute-start.17
  77.8 1.2 %collective-permute-done.17.refs_2_ = bf16[128,768]{1,0:T(8,128)(2,1)S(1)} collective-permute-done((bf16[128,768]{1,0:T(8,128)(2,1)S(1)}, bf16[128,768]{1,0:T(8,128)(2,1)S(1)}, u32[]{:S(2)}, u32[]{:S(2)}) %collective-permute-start.17) | collective-permute-done | bytes 196640 | tf_op jit(solution)/shard_map/ppermute | solution.py:582
  79.1 0.0 copy-done
  79.1 0.0 copy-done.3
  79.1 3.9 %project.5 = (f32[128,3072]{1,0:T(8,128)S(1)}, f32[8,3072]{1,0:T(8,128)S(1)}) custom-call(s32[1]{0:T(128)} %bitcast.own_ref.refs_0_, bf16[128,768]{1,0:T(8,128)(2,1)S(1)} %get-tuple-element.65.refs_1_, bf16[128,768]{1,0:T(8,128)(2,1)S(1)} %collective-permute-done.17.refs_2_, bf16[1536,3072]{1,0:T(8,128)(2,1)S(1)} %fetch.1.refs_2_.refs_3_, s32[8]{0:T(128)S(1)} %copy-done.3, ...), custom_call_target="tpu_custom_call" | custom-call | flops 1207959552 | bytes 9437184 | tf_op jit(solution)/shard_map/project/pallas_call | solution.py:547
  83.0 11.3 %collective-permute-done.18 = bf16[128,3072]{1,0:T(8,128)(2,1)S(1)} collective-permute-done((bf16[128,3072]{1,0:T(8,128)(2,1)S(1)}, bf16[128,3072]{1,0:T(8,128)(2,1)S(1)}, u32[]{:S(2)}, u32[]{:S(2)}) %collective-permute-start.18) | collective-permute-done | bytes 786464 | tf_op jit(solution)/shard_map/ppermute | solution.py:658
  94.3 1.1 %add_convert_fusion = bf16[128,3072]{1,0:T(8,128)(2,1)} fusion(f32[128,3072]{1,0:T(8,128)S(1)} %get-tuple-element.67, bf16[128,3072]{1,0:T(8,128)(2,1)S(1)} %collective-permute-done.18, f32[3072]{0:T(1024)S(1)} %bitcast.2), kind=kLoop, calls=%fused_computation | loop fusion | flops 1572864 | bytes 3158016 | tf_op jit(solution)/shard_map/convert_element_type | solution.py:663
  (12 shorter events, 0.3 us)
Async XLA Ops:
  0.0 4.5 %copy-start.4 = (bf16[128,3072]{1,0:T(8,128)(2,1)S(1)}, bf16[128,3072]{1,0:T(8,128)(2,1)}, u32[]{:S(2)}) copy-start(bf16[128,3072]{1,0:T(8,128)(2,1)} %param.9) | copy-start | bytes 2359300
  1.2 6.9 %collective-permute-start.1 = (bf16[128,512]{1,0:T(8,128)(2,1)S(1)}, bf16[128,512]{1,0:T(8,128)(2,1)S(1)}, u32[]{:S(2)}, u32[]{:S(2)}) collective-permute-start(bf16[128,512]{1,0:T(8,128)(2,1)S(1)} %pad_maximum_fusion.4), channel_id=1, source_target_pairs={{1,0},{0,1},{3,2},{2,3},{5,4},{4,5},{7,6},{6,7},{9,8},{8,9},{11,10... | collective-permute-start | bytes 393224 | tf_op jit(solution)/shard_map/ppermute | solution.py:582
  4.2 5.9 %collective-permute-start.2 = (bf16[128,512]{1,0:T(8,128)(2,1)S(1)}, bf16[128,512]{1,0:T(8,128)(2,1)S(1)}, u32[]{:S(2)}, u32[]{:S(2)}) collective-permute-start(bf16[128,512]{1,0:T(8,128)(2,1)S(1)} %pad_maximum_fusion.5), channel_id=1, source_target_pairs={{3,0},{2,1},{1,2},{0,3},{7,4},{6,5},{5,6},{4,7},{11,8},{10,9},{9,1... | collective-permute-start | bytes 393224 | tf_op jit(solution)/shard_map/ppermute | solution.py:582
  4.3 1.4 %collective-permute-start = (bf16[128,512]{1,0:T(8,128)(2,1)S(1)}, bf16[128,512]{1,0:T(8,128)(2,1)S(1)}, u32[]{:S(2)}, u32[]{:S(2)}) collective-permute-start(bf16[128,512]{1,0:T(8,128)(2,1)S(1)} %pad_maximum_fusion.3), channel_id=1, source_target_pairs={{2,0},{3,1},{0,2},{1,3},{6,4},{7,5},{4,6},{5,7},{10,8},{11,9},{8,1... | collective-permute-start | bytes 393224 | tf_op jit(solution)/shard_map/ppermute | solution.py:582
  10.2 18.0 %collective-permute-start.3 = (bf16[512,512]{1,0:T(8,128)(2,1)S(1)}, bf16[512,512]{1,0:T(8,128)(2,1)S(1)}, u32[]{:S(2)}, u32[]{:S(2)}) collective-permute-start(bf16[512,512]{1,0:T(8,128)(2,1)S(1)} %pad_maximum_fusion.refs_4_), channel_id=1, source_target_pairs={{4,0},{6,2},{0,4},{2,6},{12,8},{14,10},{8,12},{10,14},{20,16},{22,... | collective-permute-start | bytes 1572872 | tf_op jit(solution)/shard_map/ppermute | solution.py:594
  11.7 16.5 %collective-permute-start.6 = (bf16[128,1536]{1,0:T(8,128)(2,1)S(1)}, bf16[128,1536]{1,0:T(8,128)(2,1)S(1)}, u32[]{:S(2)}, u32[]{:S(2)}) collective-permute-start(bf16[128,1536]{1,0:T(8,128)(2,1)S(1)} %get-tuple-element.40), channel_id=1, source_target_pairs={{1,0},{0,1},{3,2},{2,3},{5,4},{4,5},{7,6},{6,7},{9,8},{8,9},{11,10... | collective-permute-start | bytes 1179656 | tf_op jit(solution)/shard_map/ppermute | solution.py:582
  12.7 15.3 %collective-permute-start.5 = (bf16[256,512]{1,0:T(8,128)(2,1)S(1)}, bf16[256,512]{1,0:T(8,128)(2,1)S(1)}, u32[]{:S(2)}, u32[]{:S(2)}) collective-permute-start(bf16[256,512]{1,0:T(8,128)(2,1)S(1)} %pad_maximum_fusion.1), channel_id=1, source_target_pairs={{0,16},{2,18},{4,20},{6,22},{8,24},{10,26},{12,28},{14,30},{16,0},... | collective-permute-start | bytes 786440 | tf_op jit(solution)/shard_map/ppermute | solution.py:588
  15.3 12.9 %collective-permute-start.4 = (bf16[256,512]{1,0:T(8,128)(2,1)S(1)}, bf16[256,512]{1,0:T(8,128)(2,1)S(1)}, u32[]{:S(2)}, u32[]{:S(2)}) collective-permute-start(bf16[256,512]{1,0:T(8,128)(2,1)S(1)} %pad_maximum_fusion.1), channel_id=1, source_target_pairs={{0,8},{2,10},{4,12},{6,14},{8,0},{10,2},{12,4},{14,6},{16,24},{18,... | collective-permute-start | bytes 786440 | tf_op jit(solution)/shard_map/ppermute | solution.py:588
  28.3 16.4 %collective-permute-start.10 = (bf16[512,512]{1,0:T(8,128)(2,1)S(1)}, bf16[512,512]{1,0:T(8,128)(2,1)S(1)}, u32[]{:S(2)}, u32[]{:S(2)}) collective-permute-start(bf16[512,512]{1,0:T(8,128)(2,1)S(1)} %joined.3), channel_id=1, source_target_pairs={{4,0},{6,2},{0,4},{2,6},{12,8},{14,10},{8,12},{10,14},{20,16},{22,... | collective-permute-start | bytes 1572872 | tf_op jit(solution)/shard_map/ppermute | solution.py:594
  28.9 4.3 %copy-start.1 = (s32[8,8]{1,0:T(8,128)S(1)}, s32[8,8]{1,0:T(8,128)}, u32[]{:S(2)}) copy-start(s32[8,8]{1,0:T(8,128)} %refs_2_.11) | copy-start | bytes 772
  28.9 4.3 %copy-start.2 = (s32[16]{0:T(128)S(1)}, s32[16]{0:T(128)}, u32[]{:S(2)}) copy-start(s32[16]{0:T(128)} %refs_5_.1) | copy-start | bytes 196
  28.9 3.9 %collective-permute-start.7 = (bf16[256,768]{1,0:T(8,128)(2,1)S(1)}, bf16[256,768]{1,0:T(8,128)(2,1)S(1)}, u32[]{:S(2)}, u32[]{:S(2)}) collective-permute-start(bf16[256,768]{1,0:T(8,128)(2,1)S(1)} %other_columns.1), channel_id=1, source_target_pairs={{2,0},{3,1},{0,2},{1,3},{6,4},{7,5},{4,6},{5,7},{10,8},{11,9},{8,1... | collective-permute-start | bytes 1179656 | tf_op jit(solution)/shard_map/ppermute | solution.py:582
  29.0 15.7 %collective-permute-start.9 = (bf16[256,512]{1,0:T(8,128)(2,1)S(1)}, bf16[256,512]{1,0:T(8,128)(2,1)S(1)}, u32[]{:S(2)}, u32[]{:S(2)}) collective-permute-start(bf16[256,512]{1,0:T(8,128)(2,1)S(1)} %pad_maximum_fusion.2), channel_id=1, source_target_pairs={{0,16},{2,18},{4,20},{6,22},{8,24},{10,26},{12,28},{14,30},{16,0},... | collective-permute-start | bytes 786440 | tf_op jit(solution)/shard_map/ppermute | solution.py:588
  30.3 14.3 %collective-permute-start.8 = (bf16[256,512]{1,0:T(8,128)(2,1)S(1)}, bf16[256,512]{1,0:T(8,128)(2,1)S(1)}, u32[]{:S(2)}, u32[]{:S(2)}) collective-permute-start(bf16[256,512]{1,0:T(8,128)(2,1)S(1)} %pad_maximum_fusion.2), channel_id=1, source_target_pairs={{0,8},{2,10},{4,12},{6,14},{8,0},{10,2},{12,4},{14,6},{16,24},{18,... | collective-permute-start | bytes 786440 | tf_op jit(solution)/shard_map/ppermute | solution.py:588
  39.3 13.2 %collective-permute-start.12 = (bf16[512,512]{1,0:T(8,128)(2,1)S(1)}, bf16[512,512]{1,0:T(8,128)(2,1)S(1)}, u32[]{:S(2)}, u32[]{:S(2)}) collective-permute-start(bf16[512,512]{1,0:T(8,128)(2,1)S(1)} %pad_maximum_fusion.refs_4_), channel_id=1, source_target_pairs={{8,16},{10,18},{12,20},{14,22},{16,8},{18,10},{20,12},{22,14},{9,1... | collective-permute-start | bytes 1572872 | tf_op jit(solution)/shard_map/ppermute | solution.py:588
  44.7 14.9 %collective-permute-start.11 = (bf16[512,512]{1,0:T(8,128)(2,1)S(1)}, bf16[512,512]{1,0:T(8,128)(2,1)S(1)}, u32[]{:S(2)}, u32[]{:S(2)}) collective-permute-start(bf16[512,512]{1,0:T(8,128)(2,1)S(1)} %joined.4), channel_id=1, source_target_pairs={{8,0},{10,2},{12,4},{14,6},{16,24},{18,26},{20,28},{22,30},{9,1},{... | collective-permute-start | bytes 1572872 | tf_op jit(solution)/shard_map/ppermute | solution.py:588
  46.0 13.6 %collective-permute-start.13 = (bf16[512,512]{1,0:T(8,128)(2,1)S(1)}, bf16[512,512]{1,0:T(8,128)(2,1)S(1)}, u32[]{:S(2)}, u32[]{:S(2)}) collective-permute-start(bf16[512,512]{1,0:T(8,128)(2,1)S(1)} %joined.5), channel_id=1, source_target_pairs={{4,0},{6,2},{0,4},{2,6},{12,8},{14,10},{8,12},{10,14},{20,16},{22,... | collective-permute-start | bytes 1572872 | tf_op jit(solution)/shard_map/ppermute | solution.py:594
  59.7 6.8 %collective-permute-start.14 = (bf16[256,512]{1,0:T(8,128)(2,1)S(1)}, bf16[256,512]{1,0:T(8,128)(2,1)S(1)}, u32[]{:S(2)}, u32[]{:S(2)}) collective-permute-start(bf16[256,512]{1,0:T(8,128)(2,1)S(1)} %get-tuple-element.60), channel_id=1, source_target_pairs={{4,0},{6,2},{0,4},{2,6},{12,8},{14,10},{8,12},{10,14},{20,16},{22,... | collective-permute-start | bytes 786440 | tf_op jit(solution)/shard_map/ppermute | solution.py:594
  61.3 6.8 %collective-permute-start.15 = (bf16[256,512]{1,0:T(8,128)(2,1)S(1)}, bf16[256,512]{1,0:T(8,128)(2,1)S(1)}, u32[]{:S(2)}, u32[]{:S(2)}) collective-permute-start(bf16[256,512]{1,0:T(8,128)(2,1)S(1)} %lower_half.1), channel_id=1, source_target_pairs={{0,8},{2,10},{4,12},{6,14},{8,0},{10,2},{12,4},{14,6},{16,24},{18,... | collective-permute-start | bytes 786440 | tf_op jit(solution)/shard_map/ppermute | solution.py:588
  70.7 1.8 %collective-permute-start.16 = (bf16[128,768]{1,0:T(8,128)(2,1)S(1)}, bf16[128,768]{1,0:T(8,128)(2,1)S(1)}, u32[]{:S(2)}, u32[]{:S(2)}) collective-permute-start(bf16[128,768]{1,0:T(8,128)(2,1)S(1)} %get-tuple-element.61), channel_id=1, source_target_pairs={{2,0},{3,1},{0,2},{1,3},{6,4},{7,5},{4,6},{5,7},{10,8},{11,9},{8,1... | collective-permute-start | bytes 589832 | tf_op jit(solution)/shard_map/ppermute | solution.py:582
  74.3 4.8 %copy-start = (bf16[128,3072]{1,0:T(8,128)(2,1)S(1)}, bf16[128,3072]{1,0:T(8,128)(2,1)}, u32[]{:S(2)}) copy-start(bf16[128,3072]{1,0:T(8,128)(2,1)} %refs_7_.1) | copy-start | bytes 2359300
  74.3 4.8 %copy-start.3 = (s32[8]{0:T(128)S(1)}, s32[8]{0:T(128)}, u32[]{:S(2)}) copy-start(s32[8]{0:T(128)} %refs_4_.1) | copy-start | bytes 100
  74.3 20.0 %collective-permute-start.18 = (bf16[128,3072]{1,0:T(8,128)(2,1)S(1)}, bf16[128,3072]{1,0:T(8,128)(2,1)S(1)}, u32[]{:S(2)}, u32[]{:S(2)}) collective-permute-start(bf16[128,3072]{1,0:T(8,128)(2,1)S(1)} %project.4), channel_id=1, source_target_pairs={{0,1},{1,0},{2,3},{3,2},{4,5},{5,4},{6,7},{7,6},{8,9},{9,8},{10,11... | collective-permute-start | bytes 2359304 | tf_op jit(solution)/shard_map/ppermute | solution.py:658
  77.5 1.5 %collective-permute-start.17 = (bf16[128,768]{1,0:T(8,128)(2,1)S(1)}, bf16[128,768]{1,0:T(8,128)(2,1)S(1)}, u32[]{:S(2)}, u32[]{:S(2)}) collective-permute-start(bf16[128,768]{1,0:T(8,128)(2,1)S(1)} %get-tuple-element.66), channel_id=1, source_target_pairs={{2,0},{3,1},{0,2},{1,3},{6,4},{7,5},{4,6},{5,7},{10,8},{11,9},{8,1... | collective-permute-start | bytes 589832 | tf_op jit(solution)/shard_map/ppermute | solution.py:582
where the time goes:
time: 95.4 us
  waiting for transfers between devices  37 us (39%)
  Pallas kernels  33.7 us (35%)
  starting transfers between devices  22 us (23%)
  local copies, waits for them, and re-layouts  1.26 us (1%)
  other arithmetic  1.2 us (1%)
    pallas_call x6, Pallas kernels, attend(): pl.pallas_call(kernel, out_shape=out_shape, in_specs=specs, out_specs=[vm...  21.9 us
    ppermute x7, waiting for transfers between devices, along_a(): return lax.ppermute(piece, 'seq', pairs)  18.4 us
    ppermute x7, starting transfers between devices, along_a(): return lax.ppermute(piece, 'seq', pairs)  11.9 us
    ppermute x1, waiting for transfers between devices, paired(): came_back = lax.ppermute(theirs, 'head', [(0, 1), (1, 0)])  11.3 us
    pallas_call x3, Pallas kernels, project(): pl.pallas_call(kernel, out_shape=out_shape, in_specs=specs, out_specs=[vm...  7.35 us
    ppermute x7, waiting for transfers between devices, swapped(): return lax.ppermute(piece, ('seq', 'head'), pairs)  6.82 us
    ppermute x4, starting transfers between devices, beside_of(): return lax.ppermute(piece, 'seq', pairs)  4.81 us
    ppermute x7, starting transfers between devices, swapped(): return lax.ppermute(piece, ('seq', 'head'), pairs)  4.68 us
  transfers between devices with their start and end apart: 19, of which 11 were waited for; matrix products, arithmetic and copies ran while one was open for 0% of the time, Pallas kernels for 31%

commit v1 on v0

--- a/solution.py
+++ b/solution.py
@@ -20,6 +20,7 @@
 ONES = 16
 LARGE = 1e27
 VMEM_LIMIT = 24 * 1024 * 1024
+SOME = pl.CostEstimate(flops=3000000000, bytes_accessed=1, transcendentals=0)
 LITTLE = pl.CostEstimate(flops=1, bytes_accessed=1, transcendentals=0)
 
 
@@ -326,7 +327,7 @@
         in_specs=[pl.BlockSpec(memory_space=pltpu.SMEM)] + [vmem] * (len(args) - 1),
         out_specs=[vmem] * len(shapes),
         compiler_params=pltpu.CompilerParams(vmem_limit_bytes=VMEM_LIMIT),
-        cost_estimate=LITTLE,
+        cost_estimate=SOME if name == "joined" else LITTLE,
         name=name,
     )(*args)
 
@@ -615,29 +616,29 @@
     block = jnp.concatenate([early, later], axis=0)
     qw = query_rows.shape[1] // 2
     q_own, q_other = columns(query_rows, x, qw), columns(query_rows, 1 - x, qw)
-    block, early, later, out_weight, q_own, q_other = lax.optimization_barrier(
-        (block, early, later, out_weight, q_own, q_other)
+    block, later, out_weight, q_own, q_other = lax.optimization_barrier(
+        (block, later, out_weight, q_own, q_other)
     )
     by_one, by_two = [(a, a ^ 1) for a in chips], [(a, a ^ 2) for a in chips]
     beside = beside_of(block, chips)
     next_early, far_early = along_a(early, by_one), along_a(early, by_two)
     q_came = swapped(q_other, 1, 0)
     weight = fetch(out_weight)
-    beside, next_early, far_early, q_came, weight = lax.optimization_barrier(
-        (beside, next_early, far_early, q_came, weight)
-    )
-    beside_early = beside_of(joined(own, next_early, far_early), chips)
+    both_early = joined(own, next_early, far_early)
+    later, both_early = lax.optimization_barrier((later, both_early))
+    beside, both_early, q_came, weight = lax.optimization_barrier((beside, both_early, q_came, weight))
+    beside_early = beside_of(both_early, chips)
     next_later, far_later = along_a(later, by_one), along_a(later, by_two)
     q_core = swapped(other_columns(own, [q_own, q_came]), 0, 1)
+    both_later, far = joined(own, next_later, far_later), joined(own, far_early, far_later)
+    both_later, far, q_core = lax.optimization_barrier((both_later, far, q_core))
     q = turn(own, [[q_own, q_came], [q_core]])
     (state,) = stage(None, q, [block, beside], [halves_of(0, 0, 0, 0), halves_of(1, 0, 0, 1)])
     again, state = lax.optimization_barrier((block, state))
     to_middle = along_a(again, [(1, 2), (2, 1)])
-    next_later, far_later, beside_early, state = lax.optimization_barrier(
-        (next_later, far_later, beside_early, state)
-    )
-    beside_later = beside_of(joined(own, next_later, far_later), chips)
-    to_ends = along_a(joined(own, far_early, far_later), [(1, 0), (2, 3)])
+    both_later, far, beside_early, state = lax.optimization_barrier((both_later, far, beside_early, state))
+    beside_later = beside_of(both_later, chips)
+    to_ends = along_a(far, [(1, 0), (2, 3)])
     (state,) = stage(
         state, q, [next_early, next_later, far_early, far_later],
         [halves_of((0, 1), 0, 1, 0), halves_of((2, 3), 0, 2, 0)],

time: 95.4 us -> 97.8 us (1.025); the launches traced: 95.4 us -> 95.8 us
  waiting for transfers between devices: 37 us -> 33.2 us
  starting transfers between devices: 22 us -> 25.1 us
    ppermute x7, waiting for transfers between devices: 6.82 us -> 3.25 us  [swapped(): return lax.ppermute(piece, ('seq', 'head'), pairs)]
    ppermute x4, starting transfers between devices: 4.81 us -> 5.95 us  [beside_of(): return lax.ppermute(piece, 'seq', pairs)]
  transfers between devices with their start and end apart: 19 -> 19, of which waited for: 11 -> 8; matrix products, arithmetic and copies ran while one was open for 0% -> 0% of each run, Pallas kernels for 31% -> 33%
where the time goes in v1:
time: 97.8 us; the launch traced here: 95.8 us
  Pallas kernels  34.6 us (35%)
  waiting for transfers between devices  33.2 us (34%)
  starting transfers between devices  25.1 us (26%)
  local copies, waits for them, and re-layouts  1.5 us (2%)
  other arithmetic  1.19 us (1%)
    pallas_call x6, Pallas kernels, attend(): pl.pallas_call(kernel, out_shape=out_shape, in_specs=specs, out_specs=[vm...  22.8 us
    ppermute x7, waiting for transfers between devices, along_a(): return lax.ppermute(piece, 'seq', pairs)  18.1 us
    ppermute x7, starting transfers between devices, along_a(): return lax.ppermute(piece, 'seq', pairs)  12.3 us
    ppermute x1, waiting for transfers between devices, paired(): came_back = lax.ppermute(theirs, 'head', [(0, 1), (1, 0)])  11.8 us
    pallas_call x3, Pallas kernels, project(): pl.pallas_call(kernel, out_shape=out_shape, in_specs=specs, out_specs=[vm...  7.34 us
    ppermute x4, starting transfers between devices, beside_of(): return lax.ppermute(piece, 'seq', pairs)  5.95 us
    ppermute x7, starting transfers between devices, swapped(): return lax.ppermute(piece, ('seq', 'head'), pairs)  5.28 us
    pallas_call x1, Pallas kernels, fetch(): pl.pallas_call(kernel, out_shape=pltpu.VMEM(weight.shape, weight.dtype),...  3.79 us
  transfers between devices with their start and end apart: 19, of which 8 were waited for; matrix products, arithmetic and copies ran while one was open for 0% of the time, Pallas kernels for 33%

profile of v1, /device:TPU:0, one launch (start us, length us, event | category | flops | bytes accessed | tf_op | source)
XLA Modules:
  0.0 95.8 jit_solution(4781445717094827431)
XLA Ops:
  0.0 0.0 copy-start.4
  0.0 1.2 %constant_dynamic-slice_fusion.8 = (bf16[128,256]{1,0:T(8,128)(2,1)S(1)}, bf16[128,256]{1,0:T(8,128)(2,1)S(1)}, bf16[128,256]{1,0:T(8,128)(2,1)S(1)}, bf16[128,2...) fusion(bf16[128,1024]{1,0:T(8,128)(2,1)} %param.11, ...), kind=kLoop, calls=%fused_computation.15 | loop fusion | bytes 1048592 | tf_op jit(solution)/shard_map/dynamic_slice | solution.py:563
  1.2 0.5 collective-permute-start
  1.7 2.6 %collective-permute-start.1 = (bf16[128,512]{1,0:T(8,128)(2,1)S(1)}, bf16[128,512]{1,0:T(8,128)(2,1)S(1)}, u32[]{:S(2)}, u32[]{:S(2)}) collective-permute-start(bf16[128,512]{1,0:T(8,128)(2,1)S(1)} %pad_maximum_fusion.4), channel_id=1, source_target_pairs={{1,0},{0,1},{3,2},{2,3},{5,4},{4,5},{7,6},{6,7},{9,8},{8,9},{11,10... | collective-permute-start | bytes 393224 | tf_op jit(solution)/shard_map/ppermute | solution.py:583
  4.3 0.2 collective-permute-start.2
  4.5 0.0 collective-permute-done
  4.5 2.9 %collective-permute-start.5 = (bf16[256,512]{1,0:T(8,128)(2,1)S(1)}, bf16[256,512]{1,0:T(8,128)(2,1)S(1)}, u32[]{:S(2)}, u32[]{:S(2)}) collective-permute-start(bf16[256,512]{1,0:T(8,128)(2,1)S(1)} %pad_maximum_fusion.2), channel_id=1, source_target_pairs={{0,16},{2,18},{4,20},{6,22},{8,24},{10,26},{12,28},{14,30},{16,0},... | collective-permute-start | bytes 786440 | tf_op jit(solution)/shard_map/ppermute | solution.py:589
  7.4 1.6 %collective-permute-start.4 = (bf16[256,512]{1,0:T(8,128)(2,1)S(1)}, bf16[256,512]{1,0:T(8,128)(2,1)S(1)}, u32[]{:S(2)}, u32[]{:S(2)}) collective-permute-start(bf16[256,512]{1,0:T(8,128)(2,1)S(1)} %pad_maximum_fusion.2), channel_id=1, source_target_pairs={{0,8},{2,10},{4,12},{6,14},{8,0},{10,2},{12,4},{14,6},{16,24},{18,... | collective-permute-start | bytes 786440 | tf_op jit(solution)/shard_map/ppermute | solution.py:589
  9.0 0.0 copy-done.4
  9.0 0.1 constant_dynamic-slice_fusion
  9.0 0.0 collective-permute-done.1
  9.1 2.0 %collective-permute-done.2 = bf16[128,512]{1,0:T(8,128)(2,1)S(1)} collective-permute-done((bf16[128,512]{1,0:T(8,128)(2,1)S(1)}, bf16[128,512]{1,0:T(8,128)(2,1)S(1)}, u32[]{:S(2)}, u32[]{:S(2)}) %collective-permute-start.2) | collective-permute-done | bytes 131104 | tf_op jit(solution)/shard_map/ppermute | solution.py:583
  11.1 1.6 %collective-permute-start.6 = (bf16[128,1536]{1,0:T(8,128)(2,1)S(1)}, bf16[128,1536]{1,0:T(8,128)(2,1)S(1)}, u32[]{:S(2)}, u32[]{:S(2)}) collective-permute-start(bf16[128,1536]{1,0:T(8,128)(2,1)S(1)} %get-tuple-element.44), channel_id=1, source_target_pairs={{1,0},{0,1},{3,2},{2,3},{5,4},{4,5},{7,6},{6,7},{9,8},{8,9},{11,10... | collective-permute-start | bytes 1179656 | tf_op jit(solution)/shard_map/ppermute | solution.py:583
  12.7 1.5 %collective-permute-start.3 = (bf16[512,512]{1,0:T(8,128)(2,1)S(1)}, bf16[512,512]{1,0:T(8,128)(2,1)S(1)}, u32[]{:S(2)}, u32[]{:S(2)}) collective-permute-start(bf16[512,512]{1,0:T(8,128)(2,1)S(1)} %pad_maximum_fusion.refs_4_), channel_id=1, source_target_pairs={{4,0},{6,2},{0,4},{2,6},{12,8},{14,10},{8,12},{10,14},{20,16},{22,... | collective-permute-start | bytes 1572872 | tf_op jit(solution)/shard_map/ppermute | solution.py:595
  14.2 5.7 %collective-permute-done.5.below_ref.above_ref.refs_7_ = bf16[256,512]{1,0:T(8,128)(2,1)S(1)} collective-permute-done((bf16[256,512]{1,0:T(8,128)(2,1)S(1)}, bf16[256,512]{1,0:T(8,128)(2,1)S(1)}, u32[]{:S(2)}, u32[]{:S(2)}) %collective-permute-start.5) | collective-permute-done | bytes 262176 | tf_op jit(solution)/shard_map/ppermute | solution.py:589
  19.9 0.2 collective-permute-done.4.above_ref.refs_5_
  20.1 1.4 %collective-permute-start.8 = (bf16[256,512]{1,0:T(8,128)(2,1)S(1)}, bf16[256,512]{1,0:T(8,128)(2,1)S(1)}, u32[]{:S(2)}, u32[]{:S(2)}) collective-permute-start(bf16[256,512]{1,0:T(8,128)(2,1)S(1)} %pad_maximum_fusion.1), channel_id=1, source_target_pairs={{0,16},{2,18},{4,20},{6,22},{8,24},{10,26},{12,28},{14,30},{16,0},... | collective-permute-start | bytes 786440 | tf_op jit(solution)/shard_map/ppermute | solution.py:589
  21.6 3.8 %fetch.1.refs_2_.refs_3_ = bf16[1536,3072]{1,0:T(8,128)(2,1)S(1)} custom-call(bf16[1536,3072]{1,0:T(8,128)(2,1)} %weight_ref), custom_call_target="tpu_custom_call" | custom-call | flops 1 | bytes 1 | tf_op jit(solution)/shard_map/fetch/pallas_call | solution.py:474
  25.4 2.5 %collective-permute-start.7 = (bf16[256,512]{1,0:T(8,128)(2,1)S(1)}, bf16[256,512]{1,0:T(8,128)(2,1)S(1)}, u32[]{:S(2)}, u32[]{:S(2)}) collective-permute-start(bf16[256,512]{1,0:T(8,128)(2,1)S(1)} %pad_maximum_fusion.1), channel_id=1, source_target_pairs={{0,8},{2,10},{4,12},{6,14},{8,0},{10,2},{12,4},{14,6},{16,24},{18,... | collective-permute-start | bytes 786440 | tf_op jit(solution)/shard_map/ppermute | solution.py:589
  27.9 0.0 collective-permute-done.6.refs_1_
  27.9 0.0 collective-permute-done.3.refs_5_
  27.9 0.1 collective-permute-start.9
  28.0 1.6 %collective-permute-start.10 = (bf16[512,512]{1,0:T(8,128)(2,1)S(1)}, bf16[512,512]{1,0:T(8,128)(2,1)S(1)}, u32[]{:S(2)}, u32[]{:S(2)}) collective-permute-start(bf16[512,512]{1,0:T(8,128)(2,1)S(1)} %joined.3), channel_id=1, source_target_pairs={{4,0},{6,2},{0,4},{2,6},{12,8},{14,10},{8,12},{10,14},{20,16},{22,... | collective-permute-start | bytes 1572872 | tf_op jit(solution)/shard_map/ppermute | solution.py:595
  29.6 4.9 %collective-permute-done.8.below_ref.refs_8_ = bf16[256,512]{1,0:T(8,128)(2,1)S(1)} collective-permute-done((bf16[256,512]{1,0:T(8,128)(2,1)S(1)}, bf16[256,512]{1,0:T(8,128)(2,1)S(1)}, u32[]{:S(2)}, u32[]{:S(2)}) %collective-permute-start.8) | collective-permute-done | bytes 262176 | tf_op jit(solution)/shard_map/ppermute | solution.py:589
  34.5 3.9 %collective-permute-done.7.above_ref.refs_6_ = bf16[256,512]{1,0:T(8,128)(2,1)S(1)} collective-permute-done((bf16[256,512]{1,0:T(8,128)(2,1)S(1)}, bf16[256,512]{1,0:T(8,128)(2,1)S(1)}, u32[]{:S(2)}, u32[]{:S(2)}) %collective-permute-start.7) | collective-permute-done | bytes 262176 | tf_op jit(solution)/shard_map/ppermute | solution.py:589
  38.5 0.0 copy-start.1
  38.5 0.0 copy-start.2
  38.5 0.0 collective-permute-done.9.refs_2_
  38.5 0.4 turn.1.refs_3_
  38.9 0.2 copy-done.1
  39.2 0.0 copy-done.2
  39.2 6.0 %attend.6.refs_4_ = f32[2,6,144,256]{3,2,1,0:T(8,128)S(1)} custom-call(s32[1]{0:T(128)} %bitcast.own_ref.refs_0_, s32[16]{0:T(128)S(1)} %copy-done.2, s32[8,8]{1,0:T(8,128)S(1)} %copy-done.1, bf16[2,6,256,256]{3,2,1,0:T(8,128)(2,1)S(1)} %turn.1.refs_3_, bf16[512,512]{1,0:T(8,128)(2,1)S(1)} %pad_maximum_fusion.refs_4_, ...), custom_call_target="tpu_custom_call" | custom-call | flops 1 | bytes 1 | tf_op jit(solution)/shard_map/attend/pallas_call | solution.py:442
  45.2 0.7 collective-permute-start.12
  45.9 0.0 collective-permute-done.10.refs_5_
  45.9 1.3 %collective-permute-start.11 = (bf16[512,512]{1,0:T(8,128)(2,1)S(1)}, bf16[512,512]{1,0:T(8,128)(2,1)S(1)}, u32[]{:S(2)}, u32[]{:S(2)}) collective-permute-start(bf16[512,512]{1,0:T(8,128)(2,1)S(1)} %joined.5), channel_id=1, source_target_pairs={{8,0},{10,2},{12,4},{14,6},{16,24},{18,26},{20,28},{22,30},{9,1},{... | collective-permute-start | bytes 1572872 | tf_op jit(solution)/shard_map/ppermute | solution.py:589
  47.2 1.4 %collective-permute-start.13 = (bf16[512,512]{1,0:T(8,128)(2,1)S(1)}, bf16[512,512]{1,0:T(8,128)(2,1)S(1)}, u32[]{:S(2)}, u32[]{:S(2)}) collective-permute-start(bf16[512,512]{1,0:T(8,128)(2,1)S(1)} %joined.4), channel_id=1, source_target_pairs={{4,0},{6,2},{0,4},{2,6},{12,8},{14,10},{8,12},{10,14},{20,16},{22,... | collective-permute-start | bytes 1572872 | tf_op jit(solution)/shard_map/ppermute | solution.py:595
  48.6 5.3 %attend.7.refs_4_ = f32[2,6,144,256]{3,2,1,0:T(8,128)S(1)} custom-call(s32[1]{0:T(128)} %bitcast.own_ref.refs_0_, s32[16]{0:T(128)S(1)} %copy-done.2, s32[8,8]{1,0:T(8,128)S(1)} %copy-done.1, bf16[2,6,256,256]{3,2,1,0:T(8,128)(2,1)S(1)} %turn.1.refs_3_, f32[2,6,144,256]{3,2,1,0:T(8,128)S(1)} %attend.6.refs_4_, ...), custom_call_target="tpu_custom_call" | custom-call | flops 1 | bytes 1 | tf_op jit(solution)/shard_map/attend/pallas_call | solution.py:442
  53.9 0.0 collective-permute-done.12.middle_ref
  53.9 3.7 %attend.8.refs_4_ = f32[2,6,144,256]{3,2,1,0:T(8,128)S(1)} custom-call(s32[1]{0:T(128)} %bitcast.own_ref.refs_0_, s32[16]{0:T(128)S(1)} %copy-done.2, s32[8,8]{1,0:T(8,128)S(1)} %copy-done.1, bf16[2,6,256,256]{3,2,1,0:T(8,128)(2,1)S(1)} %turn.1.refs_3_, f32[2,6,144,256]{3,2,1,0:T(8,128)S(1)} %attend.7.refs_4_, ...), custom_call_target="tpu_custom_call" | custom-call | flops 1 | bytes 1 | tf_op jit(solution)/shard_map/attend/pallas_call | solution.py:442
  57.6 3.5 %collective-permute-done.11.ends_ref = bf16[512,512]{1,0:T(8,128)(2,1)S(1)} collective-permute-done((bf16[512,512]{1,0:T(8,128)(2,1)S(1)}, bf16[512,512]{1,0:T(8,128)(2,1)S(1)}, u32[]{:S(2)}, u32[]{:S(2)}) %collective-permute-start.11) | collective-permute-done | bytes 524320 | tf_op jit(solution)/shard_map/ppermute | solution.py:589
  61.1 0.0 collective-permute-done.13.refs_5_.x_ref
  61.1 0.1 picked.1
  61.2 1.4 %collective-permute-start.14 = (bf16[256,512]{1,0:T(8,128)(2,1)S(1)}, bf16[256,512]{1,0:T(8,128)(2,1)S(1)}, u32[]{:S(2)}, u32[]{:S(2)}) collective-permute-start(bf16[256,512]{1,0:T(8,128)(2,1)S(1)} %get-tuple-element.66), channel_id=1, source_target_pairs={{4,0},{6,2},{0,4},{2,6},{12,8},{14,10},{8,12},{10,14},{20,16},{22,... | collective-permute-start | bytes 786440 | tf_op jit(solution)/shard_map/ppermute | solution.py:595
  62.6 1.9 %collective-permute-start.15 = (bf16[256,512]{1,0:T(8,128)(2,1)S(1)}, bf16[256,512]{1,0:T(8,128)(2,1)S(1)}, u32[]{:S(2)}, u32[]{:S(2)}) collective-permute-start(bf16[256,512]{1,0:T(8,128)(2,1)S(1)} %lower_half.1), channel_id=1, source_target_pairs={{0,8},{2,10},{4,12},{6,14},{8,0},{10,2},{12,4},{14,6},{16,24},{18,... | collective-permute-start | bytes 786440 | tf_op jit(solution)/shard_map/ppermute | solution.py:589
  64.5 5.4 %attend.9.refs_4_ = f32[2,6,144,256]{3,2,1,0:T(8,128)S(1)} custom-call(s32[1]{0:T(128)} %bitcast.own_ref.refs_0_, s32[16]{0:T(128)S(1)} %copy-done.2, s32[8,8]{1,0:T(8,128)S(1)} %copy-done.1, bf16[2,6,256,256]{3,2,1,0:T(8,128)(2,1)S(1)} %turn.1.refs_3_, f32[2,6,144,256]{3,2,1,0:T(8,128)S(1)} %attend.8.refs_4_, ...), custom_call_target="tpu_custom_call" | custom-call | flops 1 | bytes 1 | tf_op jit(solution)/shard_map/attend/pallas_call | solution.py:442
  70.0 0.0 collective-permute-done.14.refs_5_
  70.0 0.0 collective-permute-done.15.refs_6_
  70.0 1.2 %attend.10 = (bf16[128,768]{1,0:T(8,128)(2,1)S(1)}, bf16[128,768]{1,0:T(8,128)(2,1)S(1)}) custom-call(s32[1]{0:T(128)} %bitcast.own_ref.refs_0_, s32[16]{0:T(128)S(1)} %copy-done.2, s32[8,8]{1,0:T(8,128)S(1)} %copy-done.1, bf16[2,6,256,256]{3,2,1,0:T(8,128)(2,1)S(1)} %turn.1.refs_3_, f32[2,6,144,256]{3,2,1,0:T(8,128)S(1)} %attend.9.refs_4_, ...), custom_call_target="tpu_custom_call" | custom-call | flops 1 | bytes 1 | tf_op jit(solution)/shard_map/attend/pallas_call | solution.py:442
  71.2 0.1 collective-permute-start.16
  71.3 1.7 %project.3.refs_3_ = f32[128,3072]{1,0:T(8,128)S(1)} custom-call(s32[1]{0:T(128)} %bitcast.own_ref.refs_0_, bf16[128,768]{1,0:T(8,128)(2,1)S(1)} %get-tuple-element.69.refs_1_, bf16[1536,3072]{1,0:T(8,128)(2,1)S(1)} %fetch.1.refs_2_.refs_3_), custom_call_target="tpu_custom_call" | custom-call | flops 603979776 | bytes 4718592 | tf_op jit(solution)/shard_map/project/pallas_call | solution.py:548
  73.0 0.0 collective-permute-done.16.refs_1_
  73.0 1.7 %project.4 = bf16[128,3072]{1,0:T(8,128)(2,1)S(1)} custom-call(s32[1]{0:T(128)} %bitcast.own_ref.refs_0_, bf16[128,768]{1,0:T(8,128)(2,1)S(1)} %collective-permute-done.16.refs_1_, bf16[1536,3072]{1,0:T(8,128)(2,1)S(1)} %fetch.1.refs_2_.refs_3_, f32[128,3072]{1,0:T(8,128)S(1)} %project.3.refs_3_), custom_call_target="tpu_custom_call" | custom-call | flops 603979776 | bytes 4718592 | tf_op jit(solution)/shard_map/project/pallas_call | solution.py:548
  74.7 0.0 copy-start
  74.7 0.0 copy-start.3
  74.7 1.6 %collective-permute-start.18 = (bf16[128,3072]{1,0:T(8,128)(2,1)S(1)}, bf16[128,3072]{1,0:T(8,128)(2,1)S(1)}, u32[]{:S(2)}, u32[]{:S(2)}) collective-permute-start(bf16[128,3072]{1,0:T(8,128)(2,1)S(1)} %project.4), channel_id=1, source_target_pairs={{0,1},{1,0},{2,3},{3,2},{4,5},{5,4},{6,7},{7,6},{8,9},{9,8},{10,11... | collective-permute-start | bytes 2359304 | tf_op jit(solution)/shard_map/ppermute | solution.py:659
  76.3 1.2 %attend.11 = (bf16[128,768]{1,0:T(8,128)(2,1)S(1)}, bf16[128,768]{1,0:T(8,128)(2,1)S(1)}) custom-call(s32[1]{0:T(128)} %bitcast.own_ref.refs_0_, s32[16]{0:T(128)S(1)} %copy-done.2, s32[8,8]{1,0:T(8,128)S(1)} %copy-done.1, bf16[2,6,256,256]{3,2,1,0:T(8,128)(2,1)S(1)} %turn.1.refs_3_, f32[2,6,144,256]{3,2,1,0:T(8,128)S(1)} %attend.9.refs_4_, ...), custom_call_target="tpu_custom_call" | custom-call | flops 1 | bytes 1 | tf_op jit(solution)/shard_map/attend/pallas_call | solution.py:442
  77.5 0.3 collective-permute-start.17
  77.8 1.2 %collective-permute-done.17.refs_2_ = bf16[128,768]{1,0:T(8,128)(2,1)S(1)} collective-permute-done((bf16[128,768]{1,0:T(8,128)(2,1)S(1)}, bf16[128,768]{1,0:T(8,128)(2,1)S(1)}, u32[]{:S(2)}, u32[]{:S(2)}) %collective-permute-start.17) | collective-permute-done | bytes 196640 | tf_op jit(solution)/shard_map/ppermute | solution.py:583
  79.0 0.0 copy-done
  79.0 0.0 copy-done.3
  79.0 3.9 %project.5 = (f32[128,3072]{1,0:T(8,128)S(1)}, f32[8,3072]{1,0:T(8,128)S(1)}) custom-call(s32[1]{0:T(128)} %bitcast.own_ref.refs_0_, bf16[128,768]{1,0:T(8,128)(2,1)S(1)} %get-tuple-element.71.refs_1_, bf16[128,768]{1,0:T(8,128)(2,1)S(1)} %collective-permute-done.17.refs_2_, bf16[1536,3072]{1,0:T(8,128)(2,1)S(1)} %fetch.1.refs_2_.refs_3_, s32[8]{0:T(128)S(1)} %copy-done.3, ...), custom_call_target="tpu_custom_call" | custom-call | flops 1207959552 | bytes 9437184 | tf_op jit(solution)/shard_map/project/pallas_call | solution.py:548
  83.0 11.8 %collective-permute-done.18 = bf16[128,3072]{1,0:T(8,128)(2,1)S(1)} collective-permute-done((bf16[128,3072]{1,0:T(8,128)(2,1)S(1)}, bf16[128,3072]{1,0:T(8,128)(2,1)S(1)}, u32[]{:S(2)}, u32[]{:S(2)}) %collective-permute-start.18) | collective-permute-done | bytes 786464 | tf_op jit(solution)/shard_map/ppermute | solution.py:659
  94.7 1.1 %add_convert_fusion = bf16[128,3072]{1,0:T(8,128)(2,1)} fusion(f32[128,3072]{1,0:T(8,128)S(1)} %get-tuple-element.73, bf16[128,3072]{1,0:T(8,128)(2,1)S(1)} %collective-permute-done.18, f32[3072]{0:T(1024)S(1)} %bitcast.2), kind=kLoop, calls=%fused_computation | loop fusion | flops 1572864 | bytes 3158016 | tf_op jit(solution)/shard_map/convert_element_type | solution.py:664
  (12 shorter events, 0.3 us)
Async XLA Ops:
  0.0 9.0 %copy-start.4 = (bf16[128,3072]{1,0:T(8,128)(2,1)S(1)}, bf16[128,3072]{1,0:T(8,128)(2,1)}, u32[]{:S(2)}) copy-start(bf16[128,3072]{1,0:T(8,128)(2,1)} %param.9) | copy-start | bytes 2359300
  1.2 3.3 %collective-permute-start = (bf16[128,512]{1,0:T(8,128)(2,1)S(1)}, bf16[128,512]{1,0:T(8,128)(2,1)S(1)}, u32[]{:S(2)}, u32[]{:S(2)}) collective-permute-start(bf16[128,512]{1,0:T(8,128)(2,1)S(1)} %pad_maximum_fusion.3), channel_id=1, source_target_pairs={{2,0},{3,1},{0,2},{1,3},{6,4},{7,5},{4,6},{5,7},{10,8},{11,9},{8,1... | collective-permute-start | bytes 393224 | tf_op jit(solution)/shard_map/ppermute | solution.py:583
  1.7 7.3 %collective-permute-start.1 = (bf16[128,512]{1,0:T(8,128)(2,1)S(1)}, bf16[128,512]{1,0:T(8,128)(2,1)S(1)}, u32[]{:S(2)}, u32[]{:S(2)}) collective-permute-start(bf16[128,512]{1,0:T(8,128)(2,1)S(1)} %pad_maximum_fusion.4), channel_id=1, source_target_pairs={{1,0},{0,1},{3,2},{2,3},{5,4},{4,5},{7,6},{6,7},{9,8},{8,9},{11,10... | collective-permute-start | bytes 393224 | tf_op jit(solution)/shard_map/ppermute | solution.py:583
  4.3 6.7 %collective-permute-start.2 = (bf16[128,512]{1,0:T(8,128)(2,1)S(1)}, bf16[128,512]{1,0:T(8,128)(2,1)S(1)}, u32[]{:S(2)}, u32[]{:S(2)}) collective-permute-start(bf16[128,512]{1,0:T(8,128)(2,1)S(1)} %pad_maximum_fusion.5), channel_id=1, source_target_pairs={{3,0},{2,1},{1,2},{0,3},{7,4},{6,5},{5,6},{4,7},{11,8},{10,9},{9,1... | collective-permute-start | bytes 393224 | tf_op jit(solution)/shard_map/ppermute | solution.py:583
  4.5 15.4 %collective-permute-start.5 = (bf16[256,512]{1,0:T(8,128)(2,1)S(1)}, bf16[256,512]{1,0:T(8,128)(2,1)S(1)}, u32[]{:S(2)}, u32[]{:S(2)}) collective-permute-start(bf16[256,512]{1,0:T(8,128)(2,1)S(1)} %pad_maximum_fusion.2), channel_id=1, source_target_pairs={{0,16},{2,18},{4,20},{6,22},{8,24},{10,26},{12,28},{14,30},{16,0},... | collective-permute-start | bytes 786440 | tf_op jit(solution)/shard_map/ppermute | solution.py:589
  7.4 12.7 %collective-permute-start.4 = (bf16[256,512]{1,0:T(8,128)(2,1)S(1)}, bf16[256,512]{1,0:T(8,128)(2,1)S(1)}, u32[]{:S(2)}, u32[]{:S(2)}) collective-permute-start(bf16[256,512]{1,0:T(8,128)(2,1)S(1)} %pad_maximum_fusion.2), channel_id=1, source_target_pairs={{0,8},{2,10},{4,12},{6,14},{8,0},{10,2},{12,4},{14,6},{16,24},{18,... | collective-permute-start | bytes 786440 | tf_op jit(solution)/shard_map/ppermute | solution.py:589
  11.1 16.7 %collective-permute-start.6 = (bf16[128,1536]{1,0:T(8,128)(2,1)S(1)}, bf16[128,1536]{1,0:T(8,128)(2,1)S(1)}, u32[]{:S(2)}, u32[]{:S(2)}) collective-permute-start(bf16[128,1536]{1,0:T(8,128)(2,1)S(1)} %get-tuple-element.44), channel_id=1, source_target_pairs={{1,0},{0,1},{3,2},{2,3},{5,4},{4,5},{7,6},{6,7},{9,8},{8,9},{11,10... | collective-permute-start | bytes 1179656 | tf_op jit(solution)/shard_map/ppermute | solution.py:583
  12.7 15.1 %collective-permute-start.3 = (bf16[512,512]{1,0:T(8,128)(2,1)S(1)}, bf16[512,512]{1,0:T(8,128)(2,1)S(1)}, u32[]{:S(2)}, u32[]{:S(2)}) collective-permute-start(bf16[512,512]{1,0:T(8,128)(2,1)S(1)} %pad_maximum_fusion.refs_4_), channel_id=1, source_target_pairs={{4,0},{6,2},{0,4},{2,6},{12,8},{14,10},{8,12},{10,14},{20,16},{22,... | collective-permute-start | bytes 1572872 | tf_op jit(solution)/shard_map/ppermute | solution.py:595
  20.1 14.4 %collective-permute-start.8 = (bf16[256,512]{1,0:T(8,128)(2,1)S(1)}, bf16[256,512]{1,0:T(8,128)(2,1)S(1)}, u32[]{:S(2)}, u32[]{:S(2)}) collective-permute-start(bf16[256,512]{1,0:T(8,128)(2,1)S(1)} %pad_maximum_fusion.1), channel_id=1, source_target_pairs={{0,16},{2,18},{4,20},{6,22},{8,24},{10,26},{12,28},{14,30},{16,0},... | collective-permute-start | bytes 786440 | tf_op jit(solution)/shard_map/ppermute | solution.py:589
  25.4 13.1 %collective-permute-start.7 = (bf16[256,512]{1,0:T(8,128)(2,1)S(1)}, bf16[256,512]{1,0:T(8,128)(2,1)S(1)}, u32[]{:S(2)}, u32[]{:S(2)}) collective-permute-start(bf16[256,512]{1,0:T(8,128)(2,1)S(1)} %pad_maximum_fusion.1), channel_id=1, source_target_pairs={{0,8},{2,10},{4,12},{6,14},{8,0},{10,2},{12,4},{14,6},{16,24},{18,... | collective-permute-start | bytes 786440 | tf_op jit(solution)/shard_map/ppermute | solution.py:589
  27.9 10.6 %collective-permute-start.9 = (bf16[256,768]{1,0:T(8,128)(2,1)S(1)}, bf16[256,768]{1,0:T(8,128)(2,1)S(1)}, u32[]{:S(2)}, u32[]{:S(2)}) collective-permute-start(bf16[256,768]{1,0:T(8,128)(2,1)S(1)} %other_columns.1), channel_id=1, source_target_pairs={{2,0},{3,1},{0,2},{1,3},{6,4},{7,5},{4,6},{5,7},{10,8},{11,9},{8,1... | collective-permute-start | bytes 1179656 | tf_op jit(solution)/shard_map/ppermute | solution.py:583
  28.0 17.9 %collective-permute-start.10 = (bf16[512,512]{1,0:T(8,128)(2,1)S(1)}, bf16[512,512]{1,0:T(8,128)(2,1)S(1)}, u32[]{:S(2)}, u32[]{:S(2)}) collective-permute-start(bf16[512,512]{1,0:T(8,128)(2,1)S(1)} %joined.3), channel_id=1, source_target_pairs={{4,0},{6,2},{0,4},{2,6},{12,8},{14,10},{8,12},{10,14},{20,16},{22,... | collective-permute-start | bytes 1572872 | tf_op jit(solution)/shard_map/ppermute | solution.py:595
  38.5 0.7 copy-start.1
  38.5 0.7 copy-start.2
  45.2 8.7 %collective-permute-start.12 = (bf16[512,512]{1,0:T(8,128)(2,1)S(1)}, bf16[512,512]{1,0:T(8,128)(2,1)S(1)}, u32[]{:S(2)}, u32[]{:S(2)}) collective-permute-start(bf16[512,512]{1,0:T(8,128)(2,1)S(1)} %pad_maximum_fusion.refs_4_), channel_id=1, source_target_pairs={{8,16},{10,18},{12,20},{14,22},{16,8},{18,10},{20,12},{22,14},{9,1... | collective-permute-start | bytes 1572872 | tf_op jit(solution)/shard_map/ppermute | solution.py:589
  45.9 15.2 %collective-permute-start.11 = (bf16[512,512]{1,0:T(8,128)(2,1)S(1)}, bf16[512,512]{1,0:T(8,128)(2,1)S(1)}, u32[]{:S(2)}, u32[]{:S(2)}) collective-permute-start(bf16[512,512]{1,0:T(8,128)(2,1)S(1)} %joined.5), channel_id=1, source_target_pairs={{8,0},{10,2},{12,4},{14,6},{16,24},{18,26},{20,28},{22,30},{9,1},{... | collective-permute-start | bytes 1572872 | tf_op jit(solution)/shard_map/ppermute | solution.py:589
  47.2 13.9 %collective-permute-start.13 = (bf16[512,512]{1,0:T(8,128)(2,1)S(1)}, bf16[512,512]{1,0:T(8,128)(2,1)S(1)}, u32[]{:S(2)}, u32[]{:S(2)}) collective-permute-start(bf16[512,512]{1,0:T(8,128)(2,1)S(1)} %joined.4), channel_id=1, source_target_pairs={{4,0},{6,2},{0,4},{2,6},{12,8},{14,10},{8,12},{10,14},{20,16},{22,... | collective-permute-start | bytes 1572872 | tf_op jit(solution)/shard_map/ppermute | solution.py:595
  61.2 8.8 %collective-permute-start.14 = (bf16[256,512]{1,0:T(8,128)(2,1)S(1)}, bf16[256,512]{1,0:T(8,128)(2,1)S(1)}, u32[]{:S(2)}, u32[]{:S(2)}) collective-permute-start(bf16[256,512]{1,0:T(8,128)(2,1)S(1)} %get-tuple-element.66), channel_id=1, source_target_pairs={{4,0},{6,2},{0,4},{2,6},{12,8},{14,10},{8,12},{10,14},{20,16},{22,... | collective-permute-start | bytes 786440 | tf_op jit(solution)/shard_map/ppermute | solution.py:595
  62.6 7.4 %collective-permute-start.15 = (bf16[256,512]{1,0:T(8,128)(2,1)S(1)}, bf16[256,512]{1,0:T(8,128)(2,1)S(1)}, u32[]{:S(2)}, u32[]{:S(2)}) collective-permute-start(bf16[256,512]{1,0:T(8,128)(2,1)S(1)} %lower_half.1), channel_id=1, source_target_pairs={{0,8},{2,10},{4,12},{6,14},{8,0},{10,2},{12,4},{14,6},{16,24},{18,... | collective-permute-start | bytes 786440 | tf_op jit(solution)/shard_map/ppermute | solution.py:589
  71.2 1.8 %collective-permute-start.16 = (bf16[128,768]{1,0:T(8,128)(2,1)S(1)}, bf16[128,768]{1,0:T(8,128)(2,1)S(1)}, u32[]{:S(2)}, u32[]{:S(2)}) collective-permute-start(bf16[128,768]{1,0:T(8,128)(2,1)S(1)} %get-tuple-element.67), channel_id=1, source_target_pairs={{2,0},{3,1},{0,2},{1,3},{6,4},{7,5},{4,6},{5,7},{10,8},{11,9},{8,1... | collective-permute-start | bytes 589832 | tf_op jit(solution)/shard_map/ppermute | solution.py:583
  74.7 4.3 %copy-start = (bf16[128,3072]{1,0:T(8,128)(2,1)S(1)}, bf16[128,3072]{1,0:T(8,128)(2,1)}, u32[]{:S(2)}) copy-start(bf16[128,3072]{1,0:T(8,128)(2,1)} %refs_7_.1) | copy-start | bytes 2359300
  74.7 4.3 %copy-start.3 = (s32[8]{0:T(128)S(1)}, s32[8]{0:T(128)}, u32[]{:S(2)}) copy-start(s32[8]{0:T(128)} %refs_4_.1) | copy-start | bytes 100
  74.7 20.0 %collective-permute-start.18 = (bf16[128,3072]{1,0:T(8,128)(2,1)S(1)}, bf16[128,3072]{1,0:T(8,128)(2,1)S(1)}, u32[]{:S(2)}, u32[]{:S(2)}) collective-permute-start(bf16[128,3072]{1,0:T(8,128)(2,1)S(1)} %project.4), channel_id=1, source_target_pairs={{0,1},{1,0},{2,3},{3,2},{4,5},{5,4},{6,7},{7,6},{8,9},{9,8},{10,11... | collective-permute-start | bytes 2359304 | tf_op jit(solution)/shard_map/ppermute | solution.py:659
  77.5 1.5 %collective-permute-start.17 = (bf16[128,768]{1,0:T(8,128)(2,1)S(1)}, bf16[128,768]{1,0:T(8,128)(2,1)S(1)}, u32[]{:S(2)}, u32[]{:S(2)}) collective-permute-start(bf16[128,768]{1,0:T(8,128)(2,1)S(1)} %get-tuple-element.72), channel_id=1, source_target_pairs={{2,0},{3,1},{0,2},{1,3},{6,4},{7,5},{4,6},{5,7},{10,8},{11,9},{8,1... | collective-permute-start | bytes 589832 | tf_op jit(solution)/shard_map/ppermute | solution.py:583

commit v2 on v1

--- a/solution.py
+++ b/solution.py
@@ -624,32 +624,31 @@
     next_early, far_early = along_a(early, by_one), along_a(early, by_two)
     q_came = swapped(q_other, 1, 0)
     weight = fetch(out_weight)
+    next_early, far_early, weight = lax.optimization_barrier((next_early, far_early, weight))
     both_early = joined(own, next_early, far_early)
     later, both_early = lax.optimization_barrier((later, both_early))
-    beside, both_early, q_came, weight = lax.optimization_barrier((beside, both_early, q_came, weight))
+    beside, both_early, q_came = lax.optimization_barrier((beside, both_early, q_came))
     beside_early = beside_of(both_early, chips)
     next_later, far_later = along_a(later, by_one), along_a(later, by_two)
     q_core = swapped(other_columns(own, [q_own, q_came]), 0, 1)
     both_later, far = joined(own, next_later, far_later), joined(own, far_early, far_later)
-    both_later, far, q_core = lax.optimization_barrier((both_later, far, q_core))
+    both_later, far, again, q_core = lax.optimization_barrier((both_later, far, block, q_core))
+    to_ends = along_a(far, [(1, 0), (2, 3)])
+    to_middle = along_a(again, [(1, 2), (2, 1)])
+    both_later, beside_early = lax.optimization_barrier((both_later, beside_early))
+    beside_later = beside_of(both_later, chips)
     q = turn(own, [[q_own, q_came], [q_core]])
     (state,) = stage(None, q, [block, beside], [halves_of(0, 0, 0, 0), halves_of(1, 0, 0, 1)])
-    again, state = lax.optimization_barrier((block, state))
-    to_middle = along_a(again, [(1, 2), (2, 1)])
-    both_later, far, beside_early, state = lax.optimization_barrier((both_later, far, beside_early, state))
-    beside_later = beside_of(both_later, chips)
-    to_ends = along_a(far, [(1, 0), (2, 3)])
     (state,) = stage(
         state, q, [next_early, next_later, far_early, far_later],
         [halves_of((0, 1), 0, 1, 0), halves_of((2, 3), 0, 2, 0)],
     )
-    to_middle, state = lax.optimization_barrier((to_middle, state))
-    (state,) = stage(state, q, [beside_early], [[(0, 0, 1, 1), (0, tok, 2, 1)]])
     to_ends, to_middle, beside_later, state = lax.optimization_barrier((to_ends, to_middle, beside_later, state))
     last, last_upper = picked(own, to_ends, to_middle, n_a, n_b)
     beside_last = [beside_of(last_upper, chips), along_a(lower_half(own, beside_later), by_one)]
     (state,) = stage(
-        state, q, [beside_later, last], [[(0, 0, 1, 1), (0, tok, 2, 1)], halves_of(1, 0, 3, 0)]
+        state, q, [beside_early, beside_later, last],
+        [[(0, 0, 1, 1), (0, tok, 2, 1)], [(1, 0, 1, 1), (1, tok, 2, 1)], halves_of(2, 0, 3, 0)],
     )
     last_block = [halves_of((0, 1), 0, 3, 1)]
     kept, sent = stage(state, q, beside_last, last_block, True, 1)

time: 97.8 us -> 92.7 us (0.948); the launches traced: 95.8 us -> 92.4 us
  waiting for transfers between devices: 33.2 us -> 30.1 us
  starting transfers between devices: 25.1 us -> 22.7 us
  Pallas kernels: 34.6 us -> 36.8 us
    ppermute x7, waiting for transfers between devices: 18.1 us -> 8.09 us  [along_a(): return lax.ppermute(piece, 'seq', pairs)]
    ppermute x4, waiting for transfers between devices: 0.01 us -> 7.4 us  [beside_of(): return lax.ppermute(piece, 'seq', pairs)]
    pallas_call x6 -> x5, Pallas kernels: 22.8 us -> 25.1 us  [attend(): pl.pallas_call(kernel, out_shape=out_shape, in_specs=specs, out_specs=[vm...]
    ppermute x4, starting transfers between devices: 5.95 us -> 4.89 us  [beside_of(): return lax.ppermute(piece, 'seq', pairs)]
  transfers between devices with their start and end apart: 19 -> 19, of which waited for: 8 -> 8; matrix products, arithmetic and copies ran while one was open for 0% -> 0% of each run, Pallas kernels for 33% -> 35%
where the time goes in v2:
time: 92.7 us; the launch traced here: 92.4 us
  Pallas kernels  36.8 us (40%)
  waiting for transfers between devices  30.1 us (32%)
  starting transfers between devices  22.7 us (24%)
  local copies, waits for them, and re-layouts  1.26 us (1%)
  other arithmetic  1.22 us (1%)
    pallas_call x5, Pallas kernels, attend(): pl.pallas_call(kernel, out_shape=out_shape, in_specs=specs, out_specs=[vm...  25.1 us
    ppermute x7, starting transfers between devices, along_a(): return lax.ppermute(piece, 'seq', pairs)  12 us
    ppermute x1, waiting for transfers between devices, paired(): came_back = lax.ppermute(theirs, 'head', [(0, 1), (1, 0)])  11.4 us
    ppermute x7, waiting for transfers between devices, along_a(): return lax.ppermute(piece, 'seq', pairs)  8.09 us
    ppermute x4, waiting for transfers between devices, beside_of(): return lax.ppermute(piece, 'seq', pairs)  7.4 us
    pallas_call x3, Pallas kernels, project(): pl.pallas_call(kernel, out_shape=out_shape, in_specs=specs, out_specs=[vm...  7.33 us
    ppermute x7, starting transfers between devices, swapped(): return lax.ppermute(piece, ('seq', 'head'), pairs)  5.28 us
    ppermute x4, starting transfers between devices, beside_of(): return lax.ppermute(piece, 'seq', pairs)  4.89 us
  transfers between devices with their start and end apart: 19, of which 8 were waited for; matrix products, arithmetic and copies ran while one was open for 0% of the time, Pallas kernels for 35%

profile of v2, /device:TPU:0, one launch (start us, length us, event | category | flops | bytes accessed | tf_op | source)
XLA Modules:
  0.0 92.4 jit_solution(8185971678688662625)
XLA Ops:
  0.0 0.0 copy-start.4
  0.0 1.2 %constant_dynamic-slice_fusion.8 = (bf16[128,256]{1,0:T(8,128)(2,1)S(1)}, bf16[128,256]{1,0:T(8,128)(2,1)S(1)}, bf16[128,256]{1,0:T(8,128)(2,1)S(1)}, bf16[128,2...) fusion(bf16[128,1024]{1,0:T(8,128)(2,1)} %param.11, ...), kind=kLoop, calls=%fused_computation.15 | loop fusion | bytes 1048592 | tf_op jit(solution)/shard_map/dynamic_slice | solution.py:563
  1.2 0.5 collective-permute-start
  1.7 2.6 %collective-permute-start.1 = (bf16[128,512]{1,0:T(8,128)(2,1)S(1)}, bf16[128,512]{1,0:T(8,128)(2,1)S(1)}, u32[]{:S(2)}, u32[]{:S(2)}) collective-permute-start(bf16[128,512]{1,0:T(8,128)(2,1)S(1)} %pad_maximum_fusion.4), channel_id=1, source_target_pairs={{1,0},{0,1},{3,2},{2,3},{5,4},{4,5},{7,6},{6,7},{9,8},{8,9},{11,10... | collective-permute-start | bytes 393224 | tf_op jit(solution)/shard_map/ppermute | solution.py:583
  4.3 0.2 collective-permute-start.2
  4.5 0.0 collective-permute-done
  4.5 2.9 %collective-permute-start.5 = (bf16[256,512]{1,0:T(8,128)(2,1)S(1)}, bf16[256,512]{1,0:T(8,128)(2,1)S(1)}, u32[]{:S(2)}, u32[]{:S(2)}) collective-permute-start(bf16[256,512]{1,0:T(8,128)(2,1)S(1)} %pad_maximum_fusion.2), channel_id=1, source_target_pairs={{0,16},{2,18},{4,20},{6,22},{8,24},{10,26},{12,28},{14,30},{16,0},... | collective-permute-start | bytes 786440 | tf_op jit(solution)/shard_map/ppermute | solution.py:589
  7.4 1.6 %collective-permute-start.4 = (bf16[256,512]{1,0:T(8,128)(2,1)S(1)}, bf16[256,512]{1,0:T(8,128)(2,1)S(1)}, u32[]{:S(2)}, u32[]{:S(2)}) collective-permute-start(bf16[256,512]{1,0:T(8,128)(2,1)S(1)} %pad_maximum_fusion.2), channel_id=1, source_target_pairs={{0,8},{2,10},{4,12},{6,14},{8,0},{10,2},{12,4},{14,6},{16,24},{18,... | collective-permute-start | bytes 786440 | tf_op jit(solution)/shard_map/ppermute | solution.py:589
  9.0 0.0 copy-done.4
  9.0 0.1 constant_dynamic-slice_fusion
  9.0 0.0 collective-permute-done.1
  9.1 2.0 %collective-permute-done.2 = bf16[128,512]{1,0:T(8,128)(2,1)S(1)} collective-permute-done((bf16[128,512]{1,0:T(8,128)(2,1)S(1)}, bf16[128,512]{1,0:T(8,128)(2,1)S(1)}, u32[]{:S(2)}, u32[]{:S(2)}) %collective-permute-start.2) | collective-permute-done | bytes 131104 | tf_op jit(solution)/shard_map/ppermute | solution.py:583
  11.1 1.6 %collective-permute-start.6 = (bf16[128,1536]{1,0:T(8,128)(2,1)S(1)}, bf16[128,1536]{1,0:T(8,128)(2,1)S(1)}, u32[]{:S(2)}, u32[]{:S(2)}) collective-permute-start(bf16[128,1536]{1,0:T(8,128)(2,1)S(1)} %get-tuple-element.44), channel_id=1, source_target_pairs={{1,0},{0,1},{3,2},{2,3},{5,4},{4,5},{7,6},{6,7},{9,8},{8,9},{11,10... | collective-permute-start | bytes 1179656 | tf_op jit(solution)/shard_map/ppermute | solution.py:583
  12.7 1.5 %collective-permute-start.3 = (bf16[512,512]{1,0:T(8,128)(2,1)S(1)}, bf16[512,512]{1,0:T(8,128)(2,1)S(1)}, u32[]{:S(2)}, u32[]{:S(2)}) collective-permute-start(bf16[512,512]{1,0:T(8,128)(2,1)S(1)} %pad_maximum_fusion.refs_4_), channel_id=1, source_target_pairs={{4,0},{6,2},{0,4},{2,6},{12,8},{14,10},{8,12},{10,14},{20,16},{22,... | collective-permute-start | bytes 1572872 | tf_op jit(solution)/shard_map/ppermute | solution.py:595
  14.2 3.8 %fetch.1.refs_2_.refs_3_ = bf16[1536,3072]{1,0:T(8,128)(2,1)S(1)} custom-call(bf16[1536,3072]{1,0:T(8,128)(2,1)} %weight_ref), custom_call_target="tpu_custom_call" | custom-call | flops 1 | bytes 1 | tf_op jit(solution)/shard_map/fetch/pallas_call | solution.py:474
  18.0 1.9 %collective-permute-done.5.below_ref.above_ref.refs_7_ = bf16[256,512]{1,0:T(8,128)(2,1)S(1)} collective-permute-done((bf16[256,512]{1,0:T(8,128)(2,1)S(1)}, bf16[256,512]{1,0:T(8,128)(2,1)S(1)}, u32[]{:S(2)}, u32[]{:S(2)}) %collective-permute-start.5) | collective-permute-done | bytes 262176 | tf_op jit(solution)/shard_map/ppermute | solution.py:589
  19.9 0.2 collective-permute-done.4.above_ref.refs_5_
  20.1 1.4 %collective-permute-start.8 = (bf16[256,512]{1,0:T(8,128)(2,1)S(1)}, bf16[256,512]{1,0:T(8,128)(2,1)S(1)}, u32[]{:S(2)}, u32[]{:S(2)}) collective-permute-start(bf16[256,512]{1,0:T(8,128)(2,1)S(1)} %pad_maximum_fusion.1), channel_id=1, source_target_pairs={{0,16},{2,18},{4,20},{6,22},{8,24},{10,26},{12,28},{14,30},{16,0},... | collective-permute-start | bytes 786440 | tf_op jit(solution)/shard_map/ppermute | solution.py:589
  21.6 2.4 %collective-permute-start.7 = (bf16[256,512]{1,0:T(8,128)(2,1)S(1)}, bf16[256,512]{1,0:T(8,128)(2,1)S(1)}, u32[]{:S(2)}, u32[]{:S(2)}) collective-permute-start(bf16[256,512]{1,0:T(8,128)(2,1)S(1)} %pad_maximum_fusion.1), channel_id=1, source_target_pairs={{0,8},{2,10},{4,12},{6,14},{8,0},{10,2},{12,4},{14,6},{16,24},{18,... | collective-permute-start | bytes 786440 | tf_op jit(solution)/shard_map/ppermute | solution.py:589
  24.0 0.0 collective-permute-done.6.refs_1_
  24.0 2.8 %collective-permute-done.3.refs_5_ = bf16[512,512]{1,0:T(8,128)(2,1)S(1)} collective-permute-done((bf16[512,512]{1,0:T(8,128)(2,1)S(1)}, bf16[512,512]{1,0:T(8,128)(2,1)S(1)}, u32[]{:S(2)}, u32[]{:S(2)}) %collective-permute-start.3) | collective-permute-done | bytes 524320 | tf_op jit(solution)/shard_map/ppermute | solution.py:595
  26.8 0.1 collective-permute-start.9
  26.9 1.6 %collective-permute-start.12 = (bf16[512,512]{1,0:T(8,128)(2,1)S(1)}, bf16[512,512]{1,0:T(8,128)(2,1)S(1)}, u32[]{:S(2)}, u32[]{:S(2)}) collective-permute-start(bf16[512,512]{1,0:T(8,128)(2,1)S(1)} %joined.3), channel_id=1, source_target_pairs={{4,0},{6,2},{0,4},{2,6},{12,8},{14,10},{8,12},{10,14},{20,16},{22,... | collective-permute-start | bytes 1572872 | tf_op jit(solution)/shard_map/ppermute | solution.py:595
  28.5 6.0 %collective-permute-done.8.below_ref.refs_8_ = bf16[256,512]{1,0:T(8,128)(2,1)S(1)} collective-permute-done((bf16[256,512]{1,0:T(8,128)(2,1)S(1)}, bf16[256,512]{1,0:T(8,128)(2,1)S(1)}, u32[]{:S(2)}, u32[]{:S(2)}) %collective-permute-start.8) | collective-permute-done | bytes 262176 | tf_op jit(solution)/shard_map/ppermute | solution.py:589
  34.5 0.0 collective-permute-done.7.above_ref.refs_6_
  34.6 0.0 copy-start.1
  34.6 0.0 copy-start.2
  34.6 0.0 collective-permute-done.9.refs_2_
  34.6 1.3 %collective-permute-start.10 = (bf16[512,512]{1,0:T(8,128)(2,1)S(1)}, bf16[512,512]{1,0:T(8,128)(2,1)S(1)}, u32[]{:S(2)}, u32[]{:S(2)}) collective-permute-start(bf16[512,512]{1,0:T(8,128)(2,1)S(1)} %joined.5), channel_id=1, source_target_pairs={{8,0},{10,2},{12,4},{14,6},{16,24},{18,26},{20,28},{22,30},{9,1},{... | collective-permute-start | bytes 1572872 | tf_op jit(solution)/shard_map/ppermute | solution.py:589
  35.9 0.7 collective-permute-start.11
  36.6 4.6 %collective-permute-done.12.refs_5_ = bf16[512,512]{1,0:T(8,128)(2,1)S(1)} collective-permute-done((bf16[512,512]{1,0:T(8,128)(2,1)S(1)}, bf16[512,512]{1,0:T(8,128)(2,1)S(1)}, u32[]{:S(2)}, u32[]{:S(2)}) %collective-permute-start.12) | collective-permute-done | bytes 524320 | tf_op jit(solution)/shard_map/ppermute | solution.py:595
  41.2 1.5 %collective-permute-start.13 = (bf16[512,512]{1,0:T(8,128)(2,1)S(1)}, bf16[512,512]{1,0:T(8,128)(2,1)S(1)}, u32[]{:S(2)}, u32[]{:S(2)}) collective-permute-start(bf16[512,512]{1,0:T(8,128)(2,1)S(1)} %joined.4), channel_id=1, source_target_pairs={{4,0},{6,2},{0,4},{2,6},{12,8},{14,10},{8,12},{10,14},{20,16},{22,... | collective-permute-start | bytes 1572872 | tf_op jit(solution)/shard_map/ppermute | solution.py:595
  42.8 0.4 turn.1.refs_3_
  43.2 0.0 copy-done.1
  43.2 0.0 copy-done.2
  43.2 7.4 %attend.5.refs_4_ = f32[2,6,144,256]{3,2,1,0:T(8,128)S(1)} custom-call(s32[1]{0:T(128)} %bitcast.own_ref.refs_0_, s32[16]{0:T(128)S(1)} %copy-done.2, s32[8,8]{1,0:T(8,128)S(1)} %copy-done.1, bf16[2,6,256,256]{3,2,1,0:T(8,128)(2,1)S(1)} %turn.1.refs_3_, bf16[512,512]{1,0:T(8,128)(2,1)S(1)} %pad_maximum_fusion.refs_4_, ...), custom_call_target="tpu_custom_call" | custom-call | flops 1 | bytes 1 | tf_op jit(solution)/shard_map/attend/pallas_call | solution.py:442
  50.6 5.4 %attend.6.refs_4_ = f32[2,6,144,256]{3,2,1,0:T(8,128)S(1)} custom-call(s32[1]{0:T(128)} %bitcast.own_ref.refs_0_, s32[16]{0:T(128)S(1)} %copy-done.2, s32[8,8]{1,0:T(8,128)S(1)} %copy-done.1, bf16[2,6,256,256]{3,2,1,0:T(8,128)(2,1)S(1)} %turn.1.refs_3_, f32[2,6,144,256]{3,2,1,0:T(8,128)S(1)} %attend.5.refs_4_, ...), custom_call_target="tpu_custom_call" | custom-call | flops 1 | bytes 1 | tf_op jit(solution)/shard_map/attend/pallas_call | solution.py:442
  56.0 0.0 collective-permute-done.10.ends_ref
  56.0 0.0 collective-permute-done.11.middle_ref
  56.0 0.0 collective-permute-done.13.refs_6_.x_ref
  56.0 0.1 picked.1
  56.1 0.3 collective-permute-start.14
  56.4 1.6 %collective-permute-start.15 = (bf16[256,512]{1,0:T(8,128)(2,1)S(1)}, bf16[256,512]{1,0:T(8,128)(2,1)S(1)}, u32[]{:S(2)}, u32[]{:S(2)}) collective-permute-start(bf16[256,512]{1,0:T(8,128)(2,1)S(1)} %lower_half.1), channel_id=1, source_target_pairs={{0,8},{2,10},{4,12},{6,14},{8,0},{10,2},{12,4},{14,6},{16,24},{18,... | collective-permute-start | bytes 786440 | tf_op jit(solution)/shard_map/ppermute | solution.py:589
  58.0 6.9 %attend.7.refs_4_ = f32[2,6,144,256]{3,2,1,0:T(8,128)S(1)} custom-call(s32[1]{0:T(128)} %bitcast.own_ref.refs_0_, s32[16]{0:T(128)S(1)} %copy-done.2, s32[8,8]{1,0:T(8,128)S(1)} %copy-done.1, bf16[2,6,256,256]{3,2,1,0:T(8,128)(2,1)S(1)} %turn.1.refs_3_, f32[2,6,144,256]{3,2,1,0:T(8,128)S(1)} %attend.6.refs_4_, ...), custom_call_target="tpu_custom_call" | custom-call | flops 1 | bytes 1 | tf_op jit(solution)/shard_map/attend/pallas_call | solution.py:442
  65.0 0.0 collective-permute-done.14.refs_5_
  65.0 0.0 collective-permute-done.15.refs_6_
  65.0 2.7 %attend.8 = (bf16[128,768]{1,0:T(8,128)(2,1)S(1)}, bf16[128,768]{1,0:T(8,128)(2,1)S(1)}) custom-call(s32[1]{0:T(128)} %bitcast.own_ref.refs_0_, s32[16]{0:T(128)S(1)} %copy-done.2, s32[8,8]{1,0:T(8,128)S(1)} %copy-done.1, bf16[2,6,256,256]{3,2,1,0:T(8,128)(2,1)S(1)} %turn.1.refs_3_, f32[2,6,144,256]{3,2,1,0:T(8,128)S(1)} %attend.7.refs_4_, ...), custom_call_target="tpu_custom_call" | custom-call | flops 1 | bytes 1 | tf_op jit(solution)/shard_map/attend/pallas_call | solution.py:442
  67.8 0.1 collective-permute-start.16
  67.9 1.7 %project.3.refs_3_ = f32[128,3072]{1,0:T(8,128)S(1)} custom-call(s32[1]{0:T(128)} %bitcast.own_ref.refs_0_, bf16[128,768]{1,0:T(8,128)(2,1)S(1)} %get-tuple-element.63.refs_1_, bf16[1536,3072]{1,0:T(8,128)(2,1)S(1)} %fetch.1.refs_2_.refs_3_), custom_call_target="tpu_custom_call" | custom-call | flops 603979776 | bytes 4718592 | tf_op jit(solution)/shard_map/project/pallas_call | solution.py:548
  69.6 0.0 collective-permute-done.16.refs_1_
  69.6 1.7 %project.4 = bf16[128,3072]{1,0:T(8,128)(2,1)S(1)} custom-call(s32[1]{0:T(128)} %bitcast.own_ref.refs_0_, bf16[128,768]{1,0:T(8,128)(2,1)S(1)} %collective-permute-done.16.refs_1_, bf16[1536,3072]{1,0:T(8,128)(2,1)S(1)} %fetch.1.refs_2_.refs_3_, f32[128,3072]{1,0:T(8,128)S(1)} %project.3.refs_3_), custom_call_target="tpu_custom_call" | custom-call | flops 603979776 | bytes 4718592 | tf_op jit(solution)/shard_map/project/pallas_call | solution.py:548
  71.3 0.0 copy-start
  71.3 0.0 copy-start.3
  71.3 0.6 collective-permute-start.18
  71.9 2.6 %attend.9 = (bf16[128,768]{1,0:T(8,128)(2,1)S(1)}, bf16[128,768]{1,0:T(8,128)(2,1)S(1)}) custom-call(s32[1]{0:T(128)} %bitcast.own_ref.refs_0_, s32[16]{0:T(128)S(1)} %copy-done.2, s32[8,8]{1,0:T(8,128)S(1)} %copy-done.1, bf16[2,6,256,256]{3,2,1,0:T(8,128)(2,1)S(1)} %turn.1.refs_3_, f32[2,6,144,256]{3,2,1,0:T(8,128)S(1)} %attend.7.refs_4_, ...), custom_call_target="tpu_custom_call" | custom-call | flops 1 | bytes 1 | tf_op jit(solution)/shard_map/attend/pallas_call | solution.py:442
  74.5 0.3 collective-permute-start.17
  74.8 1.2 %collective-permute-done.17.refs_2_ = bf16[128,768]{1,0:T(8,128)(2,1)S(1)} collective-permute-done((bf16[128,768]{1,0:T(8,128)(2,1)S(1)}, bf16[128,768]{1,0:T(8,128)(2,1)S(1)}, u32[]{:S(2)}, u32[]{:S(2)}) %collective-permute-start.17) | collective-permute-done | bytes 196640 | tf_op jit(solution)/shard_map/ppermute | solution.py:583
  76.0 0.0 copy-done
  76.0 0.0 copy-done.3
  76.0 3.9 %project.5 = (f32[128,3072]{1,0:T(8,128)S(1)}, f32[8,3072]{1,0:T(8,128)S(1)}) custom-call(s32[1]{0:T(128)} %bitcast.own_ref.refs_0_, bf16[128,768]{1,0:T(8,128)(2,1)S(1)} %get-tuple-element.65.refs_1_, bf16[128,768]{1,0:T(8,128)(2,1)S(1)} %collective-permute-done.17.refs_2_, bf16[1536,3072]{1,0:T(8,128)(2,1)S(1)} %fetch.1.refs_2_.refs_3_, s32[8]{0:T(128)S(1)} %copy-done.3, ...), custom_call_target="tpu_custom_call" | custom-call | flops 1207959552 | bytes 9437184 | tf_op jit(solution)/shard_map/project/pallas_call | solution.py:548
  80.0 11.4 %collective-permute-done.18 = bf16[128,3072]{1,0:T(8,128)(2,1)S(1)} collective-permute-done((bf16[128,3072]{1,0:T(8,128)(2,1)S(1)}, bf16[128,3072]{1,0:T(8,128)(2,1)S(1)}, u32[]{:S(2)}, u32[]{:S(2)}) %collective-permute-start.18) | collective-permute-done | bytes 786464 | tf_op jit(solution)/shard_map/ppermute | solution.py:658
  91.3 1.1 %add_convert_fusion = bf16[128,3072]{1,0:T(8,128)(2,1)} fusion(f32[128,3072]{1,0:T(8,128)S(1)} %get-tuple-element.67, bf16[128,3072]{1,0:T(8,128)(2,1)S(1)} %collective-permute-done.18, f32[3072]{0:T(1024)S(1)} %bitcast.2), kind=kLoop, calls=%fused_computation | loop fusion | flops 1572864 | bytes 3158016 | tf_op jit(solution)/shard_map/convert_element_type | solution.py:663
  (12 shorter events, 0.3 us)
Async XLA Ops:
  0.0 9.0 %copy-start.4 = (bf16[128,3072]{1,0:T(8,128)(2,1)S(1)}, bf16[128,3072]{1,0:T(8,128)(2,1)}, u32[]{:S(2)}) copy-start(bf16[128,3072]{1,0:T(8,128)(2,1)} %param.9) | copy-start | bytes 2359300
  1.2 3.3 %collective-permute-start = (bf16[128,512]{1,0:T(8,128)(2,1)S(1)}, bf16[128,512]{1,0:T(8,128)(2,1)S(1)}, u32[]{:S(2)}, u32[]{:S(2)}) collective-permute-start(bf16[128,512]{1,0:T(8,128)(2,1)S(1)} %pad_maximum_fusion.3), channel_id=1, source_target_pairs={{2,0},{3,1},{0,2},{1,3},{6,4},{7,5},{4,6},{5,7},{10,8},{11,9},{8,1... | collective-permute-start | bytes 393224 | tf_op jit(solution)/shard_map/ppermute | solution.py:583
  1.7 7.3 %collective-permute-start.1 = (bf16[128,512]{1,0:T(8,128)(2,1)S(1)}, bf16[128,512]{1,0:T(8,128)(2,1)S(1)}, u32[]{:S(2)}, u32[]{:S(2)}) collective-permute-start(bf16[128,512]{1,0:T(8,128)(2,1)S(1)} %pad_maximum_fusion.4), channel_id=1, source_target_pairs={{1,0},{0,1},{3,2},{2,3},{5,4},{4,5},{7,6},{6,7},{9,8},{8,9},{11,10... | collective-permute-start | bytes 393224 | tf_op jit(solution)/shard_map/ppermute | solution.py:583
  4.3 6.7 %collective-permute-start.2 = (bf16[128,512]{1,0:T(8,128)(2,1)S(1)}, bf16[128,512]{1,0:T(8,128)(2,1)S(1)}, u32[]{:S(2)}, u32[]{:S(2)}) collective-permute-start(bf16[128,512]{1,0:T(8,128)(2,1)S(1)} %pad_maximum_fusion.5), channel_id=1, source_target_pairs={{3,0},{2,1},{1,2},{0,3},{7,4},{6,5},{5,6},{4,7},{11,8},{10,9},{9,1... | collective-permute-start | bytes 393224 | tf_op jit(solution)/shard_map/ppermute | solution.py:583
  4.5 15.4 %collective-permute-start.5 = (bf16[256,512]{1,0:T(8,128)(2,1)S(1)}, bf16[256,512]{1,0:T(8,128)(2,1)S(1)}, u32[]{:S(2)}, u32[]{:S(2)}) collective-permute-start(bf16[256,512]{1,0:T(8,128)(2,1)S(1)} %pad_maximum_fusion.2), channel_id=1, source_target_pairs={{0,16},{2,18},{4,20},{6,22},{8,24},{10,26},{12,28},{14,30},{16,0},... | collective-permute-start | bytes 786440 | tf_op jit(solution)/shard_map/ppermute | solution.py:589
  7.4 12.7 %collective-permute-start.4 = (bf16[256,512]{1,0:T(8,128)(2,1)S(1)}, bf16[256,512]{1,0:T(8,128)(2,1)S(1)}, u32[]{:S(2)}, u32[]{:S(2)}) collective-permute-start(bf16[256,512]{1,0:T(8,128)(2,1)S(1)} %pad_maximum_fusion.2), channel_id=1, source_target_pairs={{0,8},{2,10},{4,12},{6,14},{8,0},{10,2},{12,4},{14,6},{16,24},{18,... | collective-permute-start | bytes 786440 | tf_op jit(solution)/shard_map/ppermute | solution.py:589
  11.1 12.9 %collective-permute-start.6 = (bf16[128,1536]{1,0:T(8,128)(2,1)S(1)}, bf16[128,1536]{1,0:T(8,128)(2,1)S(1)}, u32[]{:S(2)}, u32[]{:S(2)}) collective-permute-start(bf16[128,1536]{1,0:T(8,128)(2,1)S(1)} %get-tuple-element.44), channel_id=1, source_target_pairs={{1,0},{0,1},{3,2},{2,3},{5,4},{4,5},{7,6},{6,7},{9,8},{8,9},{11,10... | collective-permute-start | bytes 1179656 | tf_op jit(solution)/shard_map/ppermute | solution.py:583
  12.7 14.1 %collective-permute-start.3 = (bf16[512,512]{1,0:T(8,128)(2,1)S(1)}, bf16[512,512]{1,0:T(8,128)(2,1)S(1)}, u32[]{:S(2)}, u32[]{:S(2)}) collective-permute-start(bf16[512,512]{1,0:T(8,128)(2,1)S(1)} %pad_maximum_fusion.refs_4_), channel_id=1, source_target_pairs={{4,0},{6,2},{0,4},{2,6},{12,8},{14,10},{8,12},{10,14},{20,16},{22,... | collective-permute-start | bytes 1572872 | tf_op jit(solution)/shard_map/ppermute | solution.py:595
  20.1 14.4 %collective-permute-start.8 = (bf16[256,512]{1,0:T(8,128)(2,1)S(1)}, bf16[256,512]{1,0:T(8,128)(2,1)S(1)}, u32[]{:S(2)}, u32[]{:S(2)}) collective-permute-start(bf16[256,512]{1,0:T(8,128)(2,1)S(1)} %pad_maximum_fusion.1), channel_id=1, source_target_pairs={{0,16},{2,18},{4,20},{6,22},{8,24},{10,26},{12,28},{14,30},{16,0},... | collective-permute-start | bytes 786440 | tf_op jit(solution)/shard_map/ppermute | solution.py:589
  21.6 13.0 %collective-permute-start.7 = (bf16[256,512]{1,0:T(8,128)(2,1)S(1)}, bf16[256,512]{1,0:T(8,128)(2,1)S(1)}, u32[]{:S(2)}, u32[]{:S(2)}) collective-permute-start(bf16[256,512]{1,0:T(8,128)(2,1)S(1)} %pad_maximum_fusion.1), channel_id=1, source_target_pairs={{0,8},{2,10},{4,12},{6,14},{8,0},{10,2},{12,4},{14,6},{16,24},{18,... | collective-permute-start | bytes 786440 | tf_op jit(solution)/shard_map/ppermute | solution.py:589
  26.8 7.8 %collective-permute-start.9 = (bf16[256,768]{1,0:T(8,128)(2,1)S(1)}, bf16[256,768]{1,0:T(8,128)(2,1)S(1)}, u32[]{:S(2)}, u32[]{:S(2)}) collective-permute-start(bf16[256,768]{1,0:T(8,128)(2,1)S(1)} %other_columns.1), channel_id=1, source_target_pairs={{2,0},{3,1},{0,2},{1,3},{6,4},{7,5},{4,6},{5,7},{10,8},{11,9},{8,1... | collective-permute-start | bytes 1179656 | tf_op jit(solution)/shard_map/ppermute | solution.py:583
  26.9 14.3 %collective-permute-start.12 = (bf16[512,512]{1,0:T(8,128)(2,1)S(1)}, bf16[512,512]{1,0:T(8,128)(2,1)S(1)}, u32[]{:S(2)}, u32[]{:S(2)}) collective-permute-start(bf16[512,512]{1,0:T(8,128)(2,1)S(1)} %joined.3), channel_id=1, source_target_pairs={{4,0},{6,2},{0,4},{2,6},{12,8},{14,10},{8,12},{10,14},{20,16},{22,... | collective-permute-start | bytes 1572872 | tf_op jit(solution)/shard_map/ppermute | solution.py:595
  34.6 8.6 %copy-start.1 = (s32[8,8]{1,0:T(8,128)S(1)}, s32[8,8]{1,0:T(8,128)}, u32[]{:S(2)}) copy-start(s32[8,8]{1,0:T(8,128)} %refs_2_.9) | copy-start | bytes 772
  34.6 8.6 %copy-start.2 = (s32[16]{0:T(128)S(1)}, s32[16]{0:T(128)}, u32[]{:S(2)}) copy-start(s32[16]{0:T(128)} %refs_5_.1) | copy-start | bytes 196
  34.6 21.4 %collective-permute-start.10 = (bf16[512,512]{1,0:T(8,128)(2,1)S(1)}, bf16[512,512]{1,0:T(8,128)(2,1)S(1)}, u32[]{:S(2)}, u32[]{:S(2)}) collective-permute-start(bf16[512,512]{1,0:T(8,128)(2,1)S(1)} %joined.5), channel_id=1, source_target_pairs={{8,0},{10,2},{12,4},{14,6},{16,24},{18,26},{20,28},{22,30},{9,1},{... | collective-permute-start | bytes 1572872 | tf_op jit(solution)/shard_map/ppermute | solution.py:589
  35.9 20.1 %collective-permute-start.11 = (bf16[512,512]{1,0:T(8,128)(2,1)S(1)}, bf16[512,512]{1,0:T(8,128)(2,1)S(1)}, u32[]{:S(2)}, u32[]{:S(2)}) collective-permute-start(bf16[512,512]{1,0:T(8,128)(2,1)S(1)} %pad_maximum_fusion.refs_4_), channel_id=1, source_target_pairs={{8,16},{10,18},{12,20},{14,22},{16,8},{18,10},{20,12},{22,14},{9,1... | collective-permute-start | bytes 1572872 | tf_op jit(solution)/shard_map/ppermute | solution.py:589
  41.2 14.8 %collective-permute-start.13 = (bf16[512,512]{1,0:T(8,128)(2,1)S(1)}, bf16[512,512]{1,0:T(8,128)(2,1)S(1)}, u32[]{:S(2)}, u32[]{:S(2)}) collective-permute-start(bf16[512,512]{1,0:T(8,128)(2,1)S(1)} %joined.4), channel_id=1, source_target_pairs={{4,0},{6,2},{0,4},{2,6},{12,8},{14,10},{8,12},{10,14},{20,16},{22,... | collective-permute-start | bytes 1572872 | tf_op jit(solution)/shard_map/ppermute | solution.py:595
  56.1 8.9 %collective-permute-start.14 = (bf16[256,512]{1,0:T(8,128)(2,1)S(1)}, bf16[256,512]{1,0:T(8,128)(2,1)S(1)}, u32[]{:S(2)}, u32[]{:S(2)}) collective-permute-start(bf16[256,512]{1,0:T(8,128)(2,1)S(1)} %get-tuple-element.60), channel_id=1, source_target_pairs={{4,0},{6,2},{0,4},{2,6},{12,8},{14,10},{8,12},{10,14},{20,16},{22,... | collective-permute-start | bytes 786440 | tf_op jit(solution)/shard_map/ppermute | solution.py:595
  56.4 8.6 %collective-permute-start.15 = (bf16[256,512]{1,0:T(8,128)(2,1)S(1)}, bf16[256,512]{1,0:T(8,128)(2,1)S(1)}, u32[]{:S(2)}, u32[]{:S(2)}) collective-permute-start(bf16[256,512]{1,0:T(8,128)(2,1)S(1)} %lower_half.1), channel_id=1, source_target_pairs={{0,8},{2,10},{4,12},{6,14},{8,0},{10,2},{12,4},{14,6},{16,24},{18,... | collective-permute-start | bytes 786440 | tf_op jit(solution)/shard_map/ppermute | solution.py:589
  67.8 1.8 %collective-permute-start.16 = (bf16[128,768]{1,0:T(8,128)(2,1)S(1)}, bf16[128,768]{1,0:T(8,128)(2,1)S(1)}, u32[]{:S(2)}, u32[]{:S(2)}) collective-permute-start(bf16[128,768]{1,0:T(8,128)(2,1)S(1)} %get-tuple-element.61), channel_id=1, source_target_pairs={{2,0},{3,1},{0,2},{1,3},{6,4},{7,5},{4,6},{5,7},{10,8},{11,9},{8,1... | collective-permute-start | bytes 589832 | tf_op jit(solution)/shard_map/ppermute | solution.py:583
  71.3 4.7 %copy-start = (bf16[128,3072]{1,0:T(8,128)(2,1)S(1)}, bf16[128,3072]{1,0:T(8,128)(2,1)}, u32[]{:S(2)}) copy-start(bf16[128,3072]{1,0:T(8,128)(2,1)} %refs_7_.1) | copy-start | bytes 2359300
  71.3 4.7 %copy-start.3 = (s32[8]{0:T(128)S(1)}, s32[8]{0:T(128)}, u32[]{:S(2)}) copy-start(s32[8]{0:T(128)} %refs_4_.1) | copy-start | bytes 100
  71.3 20.0 %collective-permute-start.18 = (bf16[128,3072]{1,0:T(8,128)(2,1)S(1)}, bf16[128,3072]{1,0:T(8,128)(2,1)S(1)}, u32[]{:S(2)}, u32[]{:S(2)}) collective-permute-start(bf16[128,3072]{1,0:T(8,128)(2,1)S(1)} %project.4), channel_id=1, source_target_pairs={{0,1},{1,0},{2,3},{3,2},{4,5},{5,4},{6,7},{7,6},{8,9},{9,8},{10,11... | collective-permute-start | bytes 2359304 | tf_op jit(solution)/shard_map/ppermute | solution.py:658
  74.5 1.5 %collective-permute-start.17 = (bf16[128,768]{1,0:T(8,128)(2,1)S(1)}, bf16[128,768]{1,0:T(8,128)(2,1)S(1)}, u32[]{:S(2)}, u32[]{:S(2)}) collective-permute-start(bf16[128,768]{1,0:T(8,128)(2,1)S(1)} %get-tuple-element.66), channel_id=1, source_target_pairs={{2,0},{3,1},{0,2},{1,3},{6,4},{7,5},{4,6},{5,7},{10,8},{11,9},{8,1... | collective-permute-start | bytes 589832 | tf_op jit(solution)/shard_map/ppermute | solution.py:583
